TPU v7x, 768 devices: a whole 4x8x12 slice. The times are simulated.
768 devices in a mesh: seq: 16 (over x_hi, y), rep: 48 (over x_lo, z, core).
Axes of the slice: x: 4 (x_hi: 2, x_lo: 2; x = x_hi * 2 + x_lo), y: 8, z: 12, core: 2. Of those that a mesh axis runs over, the one named last changes fastest.
Arguments:
- heads_out: bfloat16 [48, 2048, 4096], P('rep', None, 'seq'), may hold values from -6 to 6
- out_grad: bfloat16 [48, 2048, 2560], P('rep', 'seq'), may hold values from -0.125 to 0.125
- drop_mask: int32 [48], P('rep'), may hold values 0 or 1
- timestep: int32 [48], P('rep'), may hold values from 0 to 999
- error_old: bfloat16 [48, 4096, 2560], P('rep', 'seq'), may hold values from -4 to 4
- q_start: float32 [2560, 8], replicated, may hold values from -0.125 to 0.125
Outputs:
- q_new: float32 [2560, 8], replicated
- error_next: bfloat16 [48, 4096, 2560], P('rep', 'seq')
All inputs are finite; a program needn't handle non-finite values. No bound on the sum of `drop_mask` on one device may be relied on, other than what follows from the above.
Results may differ from a plain program's by a relative error of at most 0.007.
Values may be sent and summed in bfloat16 or wider, within the bound.
No kernel may reach another device: no remote copies, remote signals or barrier semaphores. Data moves between devices by JAX's collectives and lax.ppermute only.
A program may use at most 64 MiB of HBM per device.

v0:
```python
import jax
import jax.numpy as jnp
from jax import lax
from jax.sharding import PartitionSpec as P

STEPS = 1000
PROMPT = 128


highest = lax.Precision.HIGHEST


def body(heads_out, out_grad, drop_mask, timestep, error_old, q_start):
    tok_count = out_grad.shape[1]
    rank_count = q_start.shape[1]
    position = lax.axis_index("seq") * tok_count + jnp.arange(tok_count)
    keeping = jnp.logical_or(position >= PROMPT, drop_mask[0] == 1)
    scaling = 0.5 + 1.5 * timestep[0].astype(jnp.float32) / STEPS
    weights = jnp.where(keeping, 1.0, 0.0).astype(jnp.float32) * scaling
    weighted = (out_grad[0].astype(jnp.float32) * weights[:, None]).astype(jnp.bfloat16)
    head_rows = heads_out[0]
    error_rows = error_old[0].astype(jnp.float32)
    gradient = lax.dot_general(
        head_rows,
        lax.all_gather(weighted, "seq", axis=0, tiled=True),
        (((0,), (0,)), ((), ())),
        preferred_element_type=jnp.float32,
    )
    merged = gradient + error_rows
    left_part = jnp.dot(merged, q_start, precision=highest)
    left_total = lax.psum(left_part, "rep")
    columns_done = []
    for column in range(rank_count):
        vector = left_total[:, column]
        if column > 0:
            previous = jnp.stack(columns_done, axis=1)
            products = lax.psum(jnp.dot(vector, previous, precision=highest), "seq")
            vector = vector - jnp.dot(previous, products, precision=highest)
        length = lax.psum(jnp.dot(vector, vector, precision=highest), "seq")
        columns_done.append(vector / jnp.sqrt(length))
    ortho_basis = jnp.stack(columns_done, axis=1)
    right_part = jnp.dot(merged.T, ortho_basis, precision=highest)
    q_new = lax.psum(right_part, ("seq", "rep")) / lax.axis_size("rep")
    decompressed = jnp.dot(ortho_basis, q_new.T, precision=highest)
    error_next = (merged - decompressed).astype(jnp.bfloat16)[None]
    return (q_new, error_next)


def solution(mesh):
    in_specs = (
        P("rep", None, "seq"),
        P("rep", "seq", None),
        P("rep"),
        P("rep"),
        P("rep", "seq", None),
        P(),
    )
    out_specs = (P(), P("rep", "seq", None))
    return jax.shard_map(body, mesh=mesh, in_specs=in_specs, out_specs=out_specs, check_vma=False)
```

profile of v0, /device:TPU:1, one launch (start us, length us, event | category | flops | bytes accessed | tf_op | source)
XLA Modules:
  0.0 1326.5 jit_solution(6589520239357187450)
XLA Ops:
  7.2 0.0 copy-start
  7.2 0.0 copy-start.2
  7.2 0.0 all-gather.2.cloned.1.call-start
  8.7 2.1 fusion.3
  10.8 0.0 all-gather.2.cloned.1.call-update
  10.9 0.0 all-reduce.2.cloned.1.call-start
  10.9 0.0 copy-done.2
  10.9 1.4 copy.8
  12.4 0.0 copy-start.4
  12.4 174.0 %all-gather.2.cloned.1.call-done = bf16[2048,2560]{1,0:T(8,128)(2,1)} async-done(((bf16[128,2560]{1,0:T(8,128)(2,1)}), bf16[2048,2560]{1,0:T(8,128)(2,1)}) %all-gather.2.cloned.1.call-update) | async-done | bytes 10485776 | tf_op jit(solution)/shard_map/all_gather | solution.py:25
  186.4 0.0 copy-done
  186.4 7.2 fusion.1
  193.6 0.0 copy-start.1
  193.6 1.5 copy-done.1
  195.1 0.0 copy-done.4
  195.1 1.4 fusion.30
  196.5 81.7 %psum.119 = f32[256,8]{0,1:T(8,128)S(1)} all-reduce(f32[256,8]{0,1:T(8,128)S(1)} %fusion.30), channel_id=1, replica_groups=mesh['seq'=16,'rep'=48] {'rep'}, use_global_device_ids=true, to_apply=%region_0.1 | all-reduce | flops 2048 | bytes 16384 | tf_op jit(solution)/shard_map/psum | solution.py:31
  278.3 0.6 multiply_reduce_fusion.8
  278.9 32.9 %psum.120 = f32[]{:T(128)} all-reduce(f32[]{:T(128)} %multiply_reduce_fusion.8), channel_id=1, replica_groups=mesh['seq'=16,'rep'=48] {'seq'}, use_global_device_ids=true, to_apply=%region_1.2 | all-reduce | flops 1 | bytes 8 | tf_op jit(solution)/shard_map/psum | solution.py:39
  312.5 0.6 multiply_reduce_fusion.7
  313.1 30.3 %psum.121 = f32[]{:T(128)} all-reduce(f32[]{:T(128)} %multiply_reduce_fusion.7), channel_id=1, replica_groups=mesh['seq'=16,'rep'=48] {'seq'}, use_global_device_ids=true, to_apply=%region_2.3 | all-reduce | flops 1 | bytes 8 | tf_op jit(solution)/shard_map/psum | solution.py:37
  343.4 1.2 multiply_reduce_fusion.6
  344.7 31.7 %psum.122 = f32[]{:T(128)} all-reduce(f32[]{:T(128)} %multiply_reduce_fusion.6), channel_id=1, replica_groups=mesh['seq'=16,'rep'=48] {'seq'}, use_global_device_ids=true, to_apply=%region_3.4 | all-reduce | flops 1 | bytes 8 | tf_op jit(solution)/shard_map/psum | solution.py:39
  377.1 0.7 broadcast_divide_fusion.6
  377.7 0.1 convolution_bitcast_fusion.6
  377.9 30.0 %psum.123 = f32[2]{0:T(128)S(1)} all-reduce(f32[2]{0:T(128)S(1)} %convolution_bitcast_fusion.6), channel_id=1, replica_groups=mesh['seq'=16,'rep'=48] {'seq'}, use_global_device_ids=true, to_apply=%region_4.5 | all-reduce | flops 2 | bytes 16 | tf_op jit(solution)/shard_map/psum | solution.py:37
  407.9 0.1 fusion.7
  408.0 0.6 multiply_reduce_fusion.5
  408.6 32.3 %psum.124 = f32[]{:T(128)} all-reduce(f32[]{:T(128)} %get-tuple-element.14), channel_id=1, replica_groups=mesh['seq'=16,'rep'=48] {'seq'}, use_global_device_ids=true, to_apply=%region_5.6 | all-reduce | flops 1 | bytes 8 | tf_op jit(solution)/shard_map/psum | solution.py:39
  441.6 0.1 convolution_bitcast_fusion.5
  441.8 30.0 %psum.125 = f32[3]{0:T(128)S(1)} all-reduce(f32[3]{0:T(128)S(1)} %convolution_bitcast_fusion.5), channel_id=1, replica_groups=mesh['seq'=16,'rep'=48] {'seq'}, use_global_device_ids=true, to_apply=%region_6.7 | all-reduce | flops 3 | bytes 24 | tf_op jit(solution)/shard_map/psum | solution.py:37
  471.8 0.1 fusion.5
  471.9 0.6 multiply_reduce_fusion.4
  472.5 31.8 %psum.126 = f32[]{:T(128)} all-reduce(f32[]{:T(128)} %get-tuple-element.12), channel_id=1, replica_groups=mesh['seq'=16,'rep'=48] {'seq'}, use_global_device_ids=true, to_apply=%region_7.8 | all-reduce | flops 1 | bytes 8 | tf_op jit(solution)/shard_map/psum | solution.py:39
  505.0 0.1 convolution_bitcast_fusion.4
  505.1 30.0 %psum.127 = f32[4]{0:T(128)S(1)} all-reduce(f32[4]{0:T(128)S(1)} %convolution_bitcast_fusion.4), channel_id=1, replica_groups=mesh['seq'=16,'rep'=48] {'seq'}, use_global_device_ids=true, to_apply=%region_8.9 | all-reduce | flops 4 | bytes 32 | tf_op jit(solution)/shard_map/psum | solution.py:37
  535.1 0.1 fusion.6
  535.2 0.6 multiply_reduce_fusion.3
  535.9 31.7 %psum.128 = f32[]{:T(128)} all-reduce(f32[]{:T(128)} %get-tuple-element.10), channel_id=1, replica_groups=mesh['seq'=16,'rep'=48] {'seq'}, use_global_device_ids=true, to_apply=%region_9.10 | all-reduce | flops 1 | bytes 8 | tf_op jit(solution)/shard_map/psum | solution.py:39
  568.3 0.1 convolution_bitcast_fusion.3
  568.5 29.7 %psum.129 = f32[5]{0:T(128)S(1)} all-reduce(f32[5]{0:T(128)S(1)} %convolution_bitcast_fusion.3), channel_id=1, replica_groups=mesh['seq'=16,'rep'=48] {'seq'}, use_global_device_ids=true, to_apply=%region_10.11 | all-reduce | flops 5 | bytes 40 | tf_op jit(solution)/shard_map/psum | solution.py:37
  598.1 0.1 fusion.12
  598.3 0.6 multiply_reduce_fusion.2
  598.9 31.9 %psum.130 = f32[]{:T(128)} all-reduce(f32[]{:T(128)} %get-tuple-element.8), channel_id=1, replica_groups=mesh['seq'=16,'rep'=48] {'seq'}, use_global_device_ids=true, to_apply=%region_11.12 | all-reduce | flops 1 | bytes 8 | tf_op jit(solution)/shard_map/psum | solution.py:39
  631.5 0.1 convolution_bitcast_fusion.2
  631.7 29.8 %psum.131 = f32[6]{0:T(128)S(1)} all-reduce(f32[6]{0:T(128)S(1)} %convolution_bitcast_fusion.2), channel_id=1, replica_groups=mesh['seq'=16,'rep'=48] {'seq'}, use_global_device_ids=true, to_apply=%region_12.13 | all-reduce | flops 6 | bytes 48 | tf_op jit(solution)/shard_map/psum | solution.py:37
  661.5 0.1 fusion.10
  661.6 0.6 multiply_reduce_fusion.1
  662.2 32.0 %psum.132 = f32[]{:T(128)} all-reduce(f32[]{:T(128)} %get-tuple-element.6), channel_id=1, replica_groups=mesh['seq'=16,'rep'=48] {'seq'}, use_global_device_ids=true, to_apply=%region_13.14 | all-reduce | flops 1 | bytes 8 | tf_op jit(solution)/shard_map/psum | solution.py:39
  694.9 0.1 convolution_bitcast_fusion.1
  695.0 29.7 %psum.133 = f32[7]{0:T(128)S(1)} all-reduce(f32[7]{0:T(128)S(1)} %convolution_bitcast_fusion.1), channel_id=1, replica_groups=mesh['seq'=16,'rep'=48] {'seq'}, use_global_device_ids=true, to_apply=%region_14.15 | all-reduce | flops 7 | bytes 56 | tf_op jit(solution)/shard_map/psum | solution.py:37
  724.7 0.1 fusion.8
  724.8 0.6 multiply_reduce_fusion
  725.5 32.0 %psum.134 = f32[]{:T(128)} all-reduce(f32[]{:T(128)} %get-tuple-element.4), channel_id=1, replica_groups=mesh['seq'=16,'rep'=48] {'seq'}, use_global_device_ids=true, to_apply=%region_15.16 | all-reduce | flops 1 | bytes 8 | tf_op jit(solution)/shard_map/psum | solution.py:39
  758.2 4.7 fusion.31
  762.8 0.0 all-reduce.2.cloned.1.call-update
  762.9 550.3 %all-reduce.2.cloned.1.call-done = f32[2560,8]{0,1:T(8,128)} async-done(((f32[2560,8]{0,1:T(8,128)}), f32[2560,8]{0,1:T(8,128)}) %all-reduce.2.cloned.1.call-update) | async-done | bytes 81936 | tf_op jit(solution)/shard_map/psum | solution.py:43
  1313.1 0.9 broadcast_multiply_fusion
  1314.0 0.0 copy-start.3
  1314.0 4.0 fusion.2
  1318.1 1.6 copy.10
  1319.6 0.0 copy-done.3
  (13 shorter events, 0.2 us)
Async XLA Ops:
  7.2 179.2 %copy-start = (bf16[1,2048,256]{2,1,0:T(8,128)(2,1)S(1)}, bf16[1,2048,256]{2,1,0:T(8,128)(2,1)}, u32[]{:S(2)}) copy-start(bf16[1,2048,256]{2,1,0:T(8,128)(2,1)} %param.6) | copy-start | bytes 3145732
  7.2 3.7 copy-start.2
  7.2 179.2 %all-gather.2.cloned.1.call-start = ((), (), s32[]{:S(2)}) async-start(), calls=%async_computation | async-start | bytes 11141120 | tf_op jit(solution)/shard_map/all_gather | solution.py:25
  10.9 1302.3 %all-reduce.2.cloned.1.call-start = ((), (), s32[]{:S(2)}) async-start(), calls=%async_computation.1 | async-start | bytes 163840 | tf_op jit(solution)/shard_map/psum | solution.py:43
  12.4 182.8 %copy-start.4 = (f32[2560,8]{0,1:T(8,128)S(1)}, f32[2560,8]{0,1:T(8,128)}, u32[]{:S(2)}) copy-start(f32[2560,8]{0,1:T(8,128)} %param.11) | copy-start | bytes 245764
  193.6 1.5 copy-start.1
  1314.0 5.6 copy-start.3
Sparse Core Ops, SparseCore 0:
  11.8 174.5 all-gather.1
  763.0 550.0 all-reduce.1
where the time goes:
time: 1330 us
  waiting for transfers between devices  724 us (54%)
  blocking collectives  548 us (41%)
  between operations  21.2 us (2%)
  matrix products  18.9 us (1%)
    psum x1, waiting for transfers between devices, body(): q_new = lax.psum(right_part, ('seq', 'rep')) / lax.axis_size('rep')  550 us
    psum x8, blocking collectives, body(): length = lax.psum(jnp.dot(vector, vector, precision=highest), 'seq')  256 us
    psum x7, blocking collectives, body(): products = lax.psum(jnp.dot(vector, previous, precision=highest), 'seq')  209 us
    all_gather x1, waiting for transfers between devices, body(): lax.all_gather(weighted, 'seq', axis=0, tiled=True)  174 us
    psum x1, blocking collectives, body(): left_total = lax.psum(left_part, 'rep')  81.7 us
  transfers between devices with their start and end apart: 2, of which 2 were waited for; matrix products, arithmetic and copies ran while one was open for 0% of the time, Pallas kernels for 0%

commit v1 on v0

v1 whole, which is shorter than its diff:
```python
import jax
import jax.numpy as jnp
from jax import lax
from jax.sharding import Mesh, PartitionSpec as P

STEPS = 1000
PROMPT = 128
SEQ = ("xh", "y")
REP = ("xl", "z", "c")
highest = lax.Precision.HIGHEST
f32 = jnp.float32
bf16 = jnp.bfloat16


def spread(x, axes):
    n = lax.axis_size(axes)
    return lax.all_to_all(jnp.broadcast_to(x[None], (n,) + x.shape), axes, 0, 0)


def body(heads_out, out_grad, drop_mask, timestep, error_old, q_start):
    tok = out_grad.shape[1]
    dout = out_grad.shape[2]
    rank = q_start.shape[1]
    half = lax.axis_index("xh")
    position = lax.axis_index(SEQ) * tok + jnp.arange(tok)
    keeping = jnp.logical_or(position >= PROMPT, drop_mask[0] == 1)
    scaling = 0.5 + 1.5 * timestep[0].astype(f32) / STEPS
    weights = jnp.where(keeping, 1.0, 0.0).astype(f32) * scaling
    weighted = (out_grad[0].astype(f32) * weights[:, None]).astype(bf16)
    heads = heads_out[0]
    error = error_old[0]
    n_tok, feats = heads.shape
    mine = n_tok // 2

    gathered = lax.all_gather(weighted, "y", axis=0, tiled=True)
    away = lax.dynamic_slice_in_dim(heads, (1 - half) * mine, mine, 0)
    here = lax.dynamic_slice_in_dim(heads, half * mine, mine, 0)
    swap = [(0, 1), (1, 0)]
    partner = lax.ppermute(away, "xh", swap)

    q_t = q_start.T
    proj = jnp.einsum("kd,td->kt", q_t, weighted.astype(f32), precision=highest)
    proj_all = spread(proj, SEQ)
    left_part = jnp.einsum("skt,stf->kf", proj_all, heads.astype(f32).reshape(16, tok, feats), precision=highest)
    left_part += jnp.einsum("kd,fd->kf", q_t, error.astype(f32), precision=highest)
    left = jnp.sum(spread(left_part, REP), axis=0)
    token_part = jnp.einsum("kf,stf->skt", left, heads.astype(f32).reshape(16, tok, feats), precision=highest)
    token = jnp.sum(lax.all_to_all(token_part, SEQ, 0, 0), axis=0)
    right_part = jnp.dot(token, weighted.astype(f32), precision=highest)
    right_part += jnp.dot(left, error.astype(f32), precision=highest)
    gram_part = jnp.dot(left, left.T, precision=highest)
    lanes = 128
    tiles = dout // lanes
    parts = right_part.reshape(rank, tiles, lanes).transpose(1, 0, 2)
    gram_tile = jnp.pad(gram_part, ((0, 0), (0, lanes - rank)))[None]
    parts = jnp.concatenate([parts, gram_tile, jnp.zeros((32 - tiles - 1, rank, lanes), f32)], axis=0)
    group = ("xh", "y", "c")
    tile = jnp.sum(lax.all_to_all(parts, group, 0, 0), axis=0)

    gathered, tile, partner = lax.optimization_barrier((gathered, tile, partner))
    dims = (((0,), (0,)), ((), ()))
    other_sum = lax.dot_general(partner, gathered, dims, preferred_element_type=f32).astype(bf16)
    from_partner = lax.ppermute(other_sum, "xh", swap)
    own_sum = lax.dot_general(here, gathered, dims, preferred_element_type=f32)

    tile = jnp.sum(spread(tile, ("xl", "z")), axis=0)
    whole = spread(tile, group)
    reps = lax.axis_size(REP)
    gram = whole[tiles][:, :rank] / reps
    right = whole[:tiles].transpose(1, 0, 2).reshape(rank, dout)
    work = jnp.concatenate([gram, jnp.eye(rank, dtype=f32)], axis=1)
    rows = jnp.arange(rank)
    for j in range(rank):
        pivot = work[j] * lax.rsqrt(work[j, j])
        below = jnp.where(rows > j, work[:, j] / jnp.sqrt(work[j, j]), 0.0)
        work = jnp.where((rows == j)[:, None], pivot[None], work - below[:, None] * pivot[None])
    inverse = work[:, rank:]
    basis = jnp.dot(inverse, left, precision=highest)
    q_new = jnp.dot(inverse, right, precision=highest) / reps
    decompressed = jnp.einsum("kf,kd->fd", basis, q_new, precision=highest)
    merged = own_sum + from_partner.astype(f32) + error.astype(f32)
    error_next = (merged - decompressed).astype(bf16)[None]
    return (q_new.T, error_next)


def solution(mesh):
    split = Mesh(mesh.devices.reshape(2, 8, 2, 12, 2), SEQ + REP)
    in_specs = (
        P(REP, None, SEQ),
        P(REP, SEQ, None),
        P(REP),
        P(REP),
        P(REP, SEQ, None),
        P(),
    )
    out_specs = (P(), P(REP, SEQ, None))
    return jax.shard_map(body, mesh=split, in_specs=in_specs, out_specs=out_specs, check_vma=False)
```

time: 1330 us -> 178 us (0.13)
  waiting for transfers between devices: 724 us -> 50.9 us
  blocking collectives: 548 us -> 18.9 us
  starting transfers between devices: 0.08 us -> 47.4 us
    psum x1 -> x0, waiting for transfers between devices: 550 us -> none  [body(): q_new = lax.psum(right_part, ('seq', 'rep')) / lax.axis_size('rep')]
    psum x16 -> x0, blocking collectives: 548 us -> none  [the longest x8 256 us: body(): length = lax.psum(jnp.dot(vector, vector, precision=highest), 'seq')]
    all_gather x1, waiting for transfers between devices: 174 us -> 0.02 us  [body(): gathered = lax.all_gather(weighted, 'y', axis=0, tiled=True)]
    all_to_all x0 -> x5, waiting for transfers between devices: none -> 43 us  [the longest x3 24.2 us: spread(): return lax.all_to_all(jnp.broadcast_to(x[None], (n,) + x.shape), axes, 0, 0)]
    all_to_all x0 -> x5, starting transfers between devices: none -> 39.6 us  [the longest x3 31.1 us: spread(): return lax.all_to_all(jnp.broadcast_to(x[None], (n,) + x.shape), axes, 0, 0)]
    all_to_all x0 -> x1, blocking collectives: none -> 18.9 us  [spread(): return lax.all_to_all(jnp.broadcast_to(x[None], (n,) + x.shape), axes, 0, 0)]
  transfers between devices with their start and end apart: 2 -> 8, of which waited for: 2 -> 6; matrix products, arithmetic and copies ran while one was open for 0% -> 13% of each run, Pallas kernels for 0% -> 0%
where the time goes in v1:
time: 178 us; the launch traced here: 177 us
  waiting for transfers between devices  50.9 us (29%)
  starting transfers between devices  47.4 us (27%)
  between operations  26.8 us (15%)
  matrix products  19.6 us (11%)
  blocking collectives  18.9 us (11%)
  local copies, waits for them, and re-layouts  7.76 us (4%)
  other arithmetic  5.16 us (3%)
    all_to_all x3, starting transfers between devices, spread(): return lax.all_to_all(jnp.broadcast_to(x[None], (n,) + x.shape), axes, 0, 0)  31.1 us
    all_to_all x3, waiting for transfers between devices, spread(): return lax.all_to_all(jnp.broadcast_to(x[None], (n,) + x.shape), axes, 0, 0)  24.2 us
    all_to_all x1, blocking collectives, spread(): return lax.all_to_all(jnp.broadcast_to(x[None], (n,) + x.shape), axes, 0, 0)  18.9 us
    all_to_all x1, waiting for transfers between devices, body(): tile = jnp.sum(lax.all_to_all(parts, group, 0, 0), axis=0)  10.6 us
    all_to_all x1, waiting for transfers between devices, body(): token = jnp.sum(lax.all_to_all(token_part, SEQ, 0, 0), axis=0)  8.22 us
    ppermute x1, waiting for transfers between devices, body(): from_partner = lax.ppermute(other_sum, 'xh', swap)  7.88 us
    dot_general x1, matrix products, body(): own_sum = lax.dot_general(here, gathered, dims, preferred_element_type=f32)  5.68 us
    dot_general x1, matrix products, body(): lax.dot_general(partner, gathered, dims, preferred_element_type=f32)  5.26 us
  transfers between devices with their start and end apart: 8, of which 6 were waited for; matrix products, arithmetic and copies ran while one was open for 13% of the time, Pallas kernels for 0%

profile of v1, /device:TPU:1, one launch (start us, length us, event | category | flops | bytes accessed | tf_op | source)
XLA Modules:
  0.0 176.5 jit_solution(17216329800269284455)
XLA Ops:
  7.2 0.0 copy-start
  7.2 0.0 all-gather.2.cloned.1.call-start
  8.7 2.1 %fusion.4 = bf16[128,2560]{1,0:T(8,128)(2,1)} fusion(bf16[1,128,2560]{2,1,0:T(8,128)(2,1)} %param.7, f32[128]{0:T(128)S(1)} %fusion.20), kind=kLoop, calls=%fused_computation.9 | loop fusion | flops 983040 | bytes 1311232 | tf_op jit(solution)/shard_map/convert_element_type | solution.py:29
  10.8 0.0 all-gather.2.cloned.1.call-update
  10.8 1.7 convolution_bitcast_fusion.2
  12.6 18.9 %all_to_all.30 = f32[16,8,128]{2,1,0:T(8,128)S(1)} all-to-all(f32[16,8,128]{2,1,0:T(8,128)S(1)} %broadcast_in_dim.197), channel_id=1, replica_groups=mesh['xh'=2,'y'=8,'xl'=2,'z'=12,'c'=2] {'xh','y'}, dimensions={0} | all-to-all | bytes 131072 | tf_op jit(solution)/shard_map/all_to_all | solution.py:17
  31.5 0.5 convolution_bitcast_fusion.1
  32.0 0.0 copy-done.1
  32.0 1.1 fusion.10
  33.1 0.8 broadcast_in_dim.198
  33.9 17.6 %all-to-all-start.1 = ((f32[48,8,256]{2,1,0:T(8,128)}), f32[48,8,256]{2,1,0:T(8,128)S(1)}, u32[]{:S(2)}, u32[]{:S(2)}) async-start(f32[48,8,256]{2,1,0:T(8,128)} %broadcast_in_dim.198), calls=%async_computation.1 | async-start | bytes 786432 | tf_op jit(solution)/shard_map/all_to_all | solution.py:17
  51.6 0.9 dynamic-slice_bitcast_fusion
  52.4 2.9 %collective-permute-start = (bf16[1024,256]{1,0:T(8,128)(2,1)}, bf16[1024,256]{1,0:T(8,128)(2,1)}, u32[]{:S(2)}, u32[]{:S(2)}) collective-permute-start(bf16[1024,256]{1,0:T(8,128)(2,1)} %dynamic-slice_bitcast_fusion), channel_id=1, source_target_pairs={{0,384},{384,0},{1,385},{385,1},{2,386},{386,2},{3,387},{387,3},{4... | collective-permute-start | bytes 1572872 | tf_op jit(solution)/shard_map/ppermute | solution.py:39
  55.3 0.1 pad.9.clone
  55.4 13.9 %all-to-all-done.1 = f32[48,8,256]{2,1,0:T(8,128)S(1)} async-done(((f32[48,8,256]{2,1,0:T(8,128)}), f32[48,8,256]{2,1,0:T(8,128)S(1)}, u32[]{:S(2)}, u32[]{:S(2)}) %all-to-all-start.1) | async-done | bytes 393248 | tf_op jit(solution)/shard_map/all_to_all | solution.py:17
  69.3 0.1 reduce_sum.36
  69.4 1.6 convolution_bitcast_fusion
  71.0 3.5 %all-to-all-start.2 = ((f32[16,8,128]{2,1,0:T(8,128)}), f32[16,8,128]{2,1,0:T(8,128)S(1)}, u32[]{:S(2)}, u32[]{:S(2)}) async-start(f32[16,8,128]{2,1,0:T(8,128)} %convolution_bitcast_fusion), calls=%async_computation.2 | async-start | bytes 131072 | tf_op jit(solution)/shard_map/all_to_all | solution.py:48
  74.5 0.6 fusion.5
  75.1 0.1 fusion.22
  75.2 8.2 %all-to-all-done.2 = f32[16,8,128]{2,1,0:T(8,128)S(1)} async-done(((f32[16,8,128]{2,1,0:T(8,128)}), f32[16,8,128]{2,1,0:T(8,128)S(1)}, u32[]{:S(2)}, u32[]{:S(2)}) %all-to-all-start.2) | async-done | bytes 65568 | tf_op jit(solution)/shard_map/all_to_all | solution.py:48
  83.5 0.4 fusion.9
  83.8 0.8 maximum_maximum_fusion
  84.6 4.9 %all-to-all-start.3 = ((f32[32,8,128]{2,1,0:T(8,128)}), f32[32,8,128]{2,1,0:T(8,128)S(1)}, u32[]{:S(2)}, u32[]{:S(2)}) async-start(f32[32,8,128]{2,1,0:T(8,128)} %maximum_maximum_fusion), calls=%async_computation.3 | async-start | bytes 262144 | tf_op jit(solution)/shard_map/all_to_all | solution.py:58
  89.6 10.6 %all-to-all-done.3 = f32[32,8,128]{2,1,0:T(8,128)S(1)} async-done(((f32[32,8,128]{2,1,0:T(8,128)}), f32[32,8,128]{2,1,0:T(8,128)S(1)}, u32[]{:S(2)}, u32[]{:S(2)}) %all-to-all-start.3) | async-done | bytes 131104 | tf_op jit(solution)/shard_map/all_to_all | solution.py:58
  100.2 0.0 all-gather.2.cloned.1.call-done
  100.3 0.6 broadcast_in_dim.201
  100.9 6.7 %all-to-all-start.4 = ((f32[24,8,128]{2,1,0:T(8,128)}), f32[24,8,128]{2,1,0:T(8,128)S(1)}, u32[]{:S(2)}, u32[]{:S(2)}) async-start(f32[24,8,128]{2,1,0:T(8,128)} %broadcast_in_dim.201), calls=%async_computation.4 | async-start | bytes 196608 | tf_op jit(solution)/shard_map/all_to_all | solution.py:17
  107.7 9.7 %all-to-all-done.4 = f32[24,8,128]{2,1,0:T(8,128)S(1)} async-done(((f32[24,8,128]{2,1,0:T(8,128)}), f32[24,8,128]{2,1,0:T(8,128)S(1)}, u32[]{:S(2)}, u32[]{:S(2)}) %all-to-all-start.4) | async-done | bytes 98336 | tf_op jit(solution)/shard_map/all_to_all | solution.py:17
  117.4 0.7 broadcast_in_dim.202
  118.1 6.8 %all-to-all-start.5 = ((f32[32,8,128]{2,1,0:T(8,128)}), f32[32,8,128]{2,1,0:T(8,128)S(1)}, u32[]{:S(2)}, u32[]{:S(2)}) async-start(f32[32,8,128]{2,1,0:T(8,128)} %broadcast_in_dim.202), calls=%async_computation.5 | async-start | bytes 262144 | tf_op jit(solution)/shard_map/all_to_all | solution.py:17
  124.9 5.3 %convolution_convert_fusion = bf16[256,2560]{1,0:T(8,128)(2,1)} fusion(bf16[1024,256]{1,0:T(8,128)(2,1)} %collective-permute-done, bf16[1024,2560]{1,0:T(8,128)(2,1)} %all-gather.2.cloned.1.call-done), kind=kOutput, calls=%fused_computation.4 | convolution fusion | flops 1342832640 | bytes 7077888 | tf_op jit(solution)/shard_map/dot_general | solution.py:62
  130.1 4.9 %collective-permute-start.1 = (bf16[256,2560]{1,0:T(8,128)(2,1)}, bf16[256,2560]{1,0:T(8,128)(2,1)}, u32[]{:S(2)}, u32[]{:S(2)}) collective-permute-start(bf16[256,2560]{1,0:T(8,128)(2,1)} %convolution_convert_fusion), channel_id=1, source_target_pairs={{0,384},{384,0},{1,385},{385,1},{2,386},{386,2},{3,387},{387,3},{4... | collective-permute-start | bytes 3932168 | tf_op jit(solution)/shard_map/ppermute | solution.py:63
  135.0 0.5 all-to-all-done.5
  135.6 0.5 slice.95
  137.4 0.1 select_reduce_fusion.7
  137.6 0.1 pad_maximum_fusion
  137.6 0.1 subtract_select_fusion.7
  137.7 0.6 slice.98
  139.7 0.2 select_reduce_fusion.6
  139.9 0.1 subtract_select_fusion.6
  140.0 0.6 slice.101
  142.0 0.2 select_reduce_fusion.5
  142.1 0.1 subtract_select_fusion.5
  142.2 0.6 slice.104
  144.2 0.2 select_reduce_fusion.4
  144.4 0.1 subtract_select_fusion.4
  144.5 0.6 slice.107
  146.4 0.2 select_reduce_fusion.3
  146.6 0.1 subtract_select_fusion.3
  146.7 0.6 slice.110
  148.7 0.2 select_reduce_fusion.2
  148.9 0.1 subtract_select_fusion.2
  149.0 0.6 slice.113
  150.9 0.2 select_reduce_fusion.1
  151.1 0.1 subtract_select_fusion.1
  151.2 0.6 slice.116
  153.2 0.1 select_reduce_fusion
  153.3 0.1 subtract_select_fusion
  153.4 0.2 fusion.17
  153.6 0.3 convolution_multiply_fusion
  153.9 2.2 %fusion.23 = f32[256,2560]{1,0:T(8,128)S(1)} fusion(f32[8,256]{1,0:T(8,128)S(1)} %fusion.17, f32[8,2560]{1,0:T(8,128)S(1)} %convolution_multiply_fusion), kind=kOutput, calls=%fused_computation.78 | convolution fusion | flops 62914560 | bytes 2711552 | tf_op jit(solution)/shard_map/kf,kd->fd/dot_general | solution.py:80
  156.1 7.9 %collective-permute-done.1 = bf16[256,2560]{1,0:T(8,128)(2,1)} collective-permute-done((bf16[256,2560]{1,0:T(8,128)(2,1)}, bf16[256,2560]{1,0:T(8,128)(2,1)}, u32[]{:S(2)}, u32[]{:S(2)}) %collective-permute-start.1) | collective-permute-done | bytes 1310752 | tf_op jit(solution)/shard_map/ppermute | solution.py:63
  164.0 5.7 %fusion.3 = bf16[1,256,2560]{2,1,0:T(8,128)(2,1)} fusion(f32[256,2560]{1,0:T(8,128)S(1)} %fusion.23, bf16[1024,2560]{1,0:T(8,128)(2,1)} %all-gather.2.cloned.1.call-done, bf16[256,2560]{1,0:T(8,128)(2,1)} %collective-permute-done.1, bf16[1,256,2560]{2,1,0:T(8,128)(2,1)S(1)} %copy-done.1, bf16[1,2048,256]{2,1,0:T(8,128)(2,1)S(1)} %copy-done, s32[]{:T(128)S(6)} %select_n.90), kind=kOutput, calls=%fused_computation.5 | convolution fusion | flops 1346109440 | bytes 12320772 | tf_op jit(solution)/shard_map/dot_general | solution.py:64
  (35 shorter events, 0.3 us)
Async XLA Ops:
  7.2 24.3 %copy-start = (bf16[1,2048,256]{2,1,0:T(8,128)(2,1)S(1)}, bf16[1,2048,256]{2,1,0:T(8,128)(2,1)}, u32[]{:S(2)}) copy-start(bf16[1,2048,256]{2,1,0:T(8,128)(2,1)} %param.6) | copy-start | bytes 3145732
  7.2 24.8 %copy-start.3 = (f32[2560,8]{0,1:T(8,128)S(1)}, f32[2560,8]{0,1:T(8,128)}, u32[]{:S(2)}) copy-start(f32[2560,8]{0,1:T(8,128)} %param.11) | copy-start | bytes 245764
  7.2 24.8 %copy-start.1 = (bf16[1,256,2560]{2,1,0:T(8,128)(2,1)S(1)}, bf16[1,256,2560]{2,1,0:T(8,128)(2,1)}, u32[]{:S(2)}) copy-start(bf16[1,256,2560]{2,1,0:T(8,128)(2,1)} %param.10) | copy-start | bytes 3932164
  7.2 93.0 %all-gather.2.cloned.1.call-start = ((), (), s32[]{:S(2)}) async-start(), calls=%async_computation.6 | async-start | bytes 5898240 | tf_op jit(solution)/shard_map/all_gather | solution.py:35
  33.1 50.4 %copy-start.2 = (bf16[128,2560]{1,0:T(8,128)(2,1)S(1)}, bf16[128,2560]{1,0:T(8,128)(2,1)}, u32[]{:S(2)}) copy-start(bf16[128,2560]{1,0:T(8,128)(2,1)} %fusion.4) | copy-start | bytes 1966084
  33.9 35.4 %all-to-all-start.1 = ((f32[48,8,256]{2,1,0:T(8,128)}), f32[48,8,256]{2,1,0:T(8,128)S(1)}, u32[]{:S(2)}, u32[]{:S(2)}) async-start(f32[48,8,256]{2,1,0:T(8,128)} %broadcast_in_dim.198), calls=%async_computation.1 | async-start | bytes 786432 | tf_op jit(solution)/shard_map/all_to_all | solution.py:17
  52.4 47.8 %collective-permute-start = (bf16[1024,256]{1,0:T(8,128)(2,1)}, bf16[1024,256]{1,0:T(8,128)(2,1)}, u32[]{:S(2)}, u32[]{:S(2)}) collective-permute-start(bf16[1024,256]{1,0:T(8,128)(2,1)} %dynamic-slice_bitcast_fusion), channel_id=1, source_target_pairs={{0,384},{384,0},{1,385},{385,1},{2,386},{386,2},{3,387},{387,3},{4... | collective-permute-start | bytes 1572872 | tf_op jit(solution)/shard_map/ppermute | solution.py:39
  71.0 12.5 %all-to-all-start.2 = ((f32[16,8,128]{2,1,0:T(8,128)}), f32[16,8,128]{2,1,0:T(8,128)S(1)}, u32[]{:S(2)}, u32[]{:S(2)}) async-start(f32[16,8,128]{2,1,0:T(8,128)} %convolution_bitcast_fusion), calls=%async_computation.2 | async-start | bytes 131072 | tf_op jit(solution)/shard_map/all_to_all | solution.py:48
  84.6 15.6 %all-to-all-start.3 = ((f32[32,8,128]{2,1,0:T(8,128)}), f32[32,8,128]{2,1,0:T(8,128)S(1)}, u32[]{:S(2)}, u32[]{:S(2)}) async-start(f32[32,8,128]{2,1,0:T(8,128)} %maximum_maximum_fusion), calls=%async_computation.3 | async-start | bytes 262144 | tf_op jit(solution)/shard_map/all_to_all | solution.py:58
  100.9 16.5 %all-to-all-start.4 = ((f32[24,8,128]{2,1,0:T(8,128)}), f32[24,8,128]{2,1,0:T(8,128)S(1)}, u32[]{:S(2)}, u32[]{:S(2)}) async-start(f32[24,8,128]{2,1,0:T(8,128)} %broadcast_in_dim.201), calls=%async_computation.4 | async-start | bytes 196608 | tf_op jit(solution)/shard_map/all_to_all | solution.py:17
  118.1 17.5 %all-to-all-start.5 = ((f32[32,8,128]{2,1,0:T(8,128)}), f32[32,8,128]{2,1,0:T(8,128)S(1)}, u32[]{:S(2)}, u32[]{:S(2)}) async-start(f32[32,8,128]{2,1,0:T(8,128)} %broadcast_in_dim.202), calls=%async_computation.5 | async-start | bytes 262144 | tf_op jit(solution)/shard_map/all_to_all | solution.py:17
  130.1 33.9 %collective-permute-start.1 = (bf16[256,2560]{1,0:T(8,128)(2,1)}, bf16[256,2560]{1,0:T(8,128)(2,1)}, u32[]{:S(2)}, u32[]{:S(2)}) collective-permute-start(bf16[256,2560]{1,0:T(8,128)(2,1)} %convolution_convert_fusion), channel_id=1, source_target_pairs={{0,384},{384,0},{1,385},{385,1},{2,386},{386,2},{3,387},{387,3},{4... | collective-permute-start | bytes 3932168 | tf_op jit(solution)/shard_map/ppermute | solution.py:63
  153.9 15.8 %copy-start.4 = (f32[8,2560]{1,0:T(8,128)}, f32[8,2560]{1,0:T(8,128)S(1)}, u32[]{:S(2)}) copy-start(f32[8,2560]{1,0:T(8,128)S(1)} %convolution_multiply_fusion) | copy-start | bytes 245764
Sparse Core Ops, SparseCore 0:
  11.0 78.6 all-gather.1

commit v2 on v1

v2 whole, which is shorter than its diff:
```python
import functools

import jax
import jax.numpy as jnp
from jax import lax
from jax.experimental import pallas as pl
from jax.experimental.pallas import tpu as pltpu
from jax.sharding import Mesh, PartitionSpec as P

STEPS = 1000
PROMPT = 128
SEQ = ("xh", "y")
REP = ("xl", "z", "c")
PAIR = ("xl", "z")
GROUP = ("xh", "y", "c")
LANES = 128
highest = lax.Precision.HIGHEST
f32 = jnp.float32
bf16 = jnp.bfloat16
VMEM = pl.BlockSpec(memory_space=pltpu.VMEM)
SMEM = pl.BlockSpec(memory_space=pltpu.SMEM)
NT = (((1,), (1,)), ((), ()))
TN = (((0,), (0,)), ((), ()))


def pieces(x):
    first = x.astype(bf16).astype(f32)
    rest = x - first
    second = rest.astype(bf16).astype(f32)
    return first, second, rest - second


def stacked(x):
    return jnp.concatenate(pieces(x) + (jnp.zeros_like(x),), axis=0).astype(bf16)


def folded(x):
    return x[0:8] + x[8:16] + x[16:24]


def call(kernel, outs, ins, flops, args):
    size = lambda a: a.size * a.dtype.itemsize
    moved = sum(size(a) for a in args) + sum(size(a) for a in outs)
    return pl.pallas_call(
        kernel,
        out_shape=outs,
        in_specs=ins,
        out_specs=[VMEM] * len(outs),
        cost_estimate=pl.CostEstimate(flops=flops, bytes_accessed=moved, transcendentals=0),
    )(*args)


def arr(shape, dtype):
    return jax.ShapeDtypeStruct(shape, dtype)


def weigh_kernel(drop_ref, step_ref, grad_ref, q_ref, weighted_ref, proj_ref):
    tok = grad_ref.shape[0]
    place = lax.axis_index("xh") * lax.axis_size("y") + lax.axis_index("y")
    position = place * tok + lax.broadcasted_iota(jnp.int32, (tok, 1), 0)
    drop = jnp.full((tok, 1), drop_ref[0], jnp.int32)
    step = jnp.full((tok, 1), step_ref[0], jnp.int32).astype(f32)
    keeping = jnp.logical_or(position >= PROMPT, drop == 1)
    weights = jnp.where(keeping, 0.5 + 1.5 * step / STEPS, 0.0)
    weighted = (grad_ref[...].astype(f32) * weights).astype(bf16)
    weighted_ref[...] = weighted
    proj = folded(lax.dot_general(stacked(q_ref[...]), weighted, NT, preferred_element_type=f32))
    for s in range(proj_ref.shape[0]):
        proj_ref[s] = proj


def error_left_kernel(q_ref, error_ref, out_ref):
    out_ref[...] = folded(lax.dot_general(stacked(q_ref[...]), error_ref[...], NT, preferred_element_type=f32))


def left_kernel(proj_ref, heads_ref, first_ref, out_ref):
    n, _, tok = proj_ref.shape
    proj = jnp.concatenate([proj_ref[s] for s in range(n)], axis=1)
    left = folded(jnp.dot(stacked(proj), heads_ref[...], preferred_element_type=f32)) + first_ref[...]
    for r in range(out_ref.shape[0]):
        out_ref[r] = left


def token_kernel(parts_ref, heads_ref, left_ref, out_ref):
    left = jnp.sum(parts_ref[...], axis=0)
    left_ref[...] = left
    token = folded(lax.dot_general(stacked(left), heads_ref[...], NT, preferred_element_type=f32))
    for s in range(out_ref.shape[0]):
        out_ref[s] = token[:, s * LANES:(s + 1) * LANES]


def error_right_kernel(left_ref, error_ref, right_ref, gram_ref):
    left = left_ref[...]
    right_ref[...] = folded(jnp.dot(stacked(left), error_ref[...], preferred_element_type=f32))
    rows = jnp.concatenate([left, jnp.zeros((LANES - 8, left.shape[1]), f32)], axis=0)
    gram_ref[...] = lax.dot_general(left, rows, NT, precision=highest, preferred_element_type=f32)


def right_kernel(token_ref, weighted_ref, right_ref, gram_ref, out_ref):
    token = jnp.sum(token_ref[...], axis=0)
    right = folded(jnp.dot(stacked(token), weighted_ref[...], preferred_element_type=f32)) + right_ref[...]
    tiles = right.shape[1] // LANES
    for t in range(tiles):
        out_ref[t] = right[:, t * LANES:(t + 1) * LANES]
    out_ref[tiles] = gram_ref[...]
    for t in range(tiles + 1, out_ref.shape[0]):
        out_ref[t] = jnp.zeros(out_ref.shape[1:], f32)


def sum_kernel(parts_ref, out_ref):
    total = jnp.sum(parts_ref[...], axis=0)
    for r in range(out_ref.shape[0]):
        out_ref[r] = total


def final_kernel(reps, gram_ref, whole_ref, left_ref, merged_ref, partner_ref, q_ref, out_ref, inverse, basis):
    @pl.when(pl.program_id(0) == 0)
    def _():
        rows = lax.broadcasted_iota(jnp.int32, (8, LANES), 0)
        lanes = lax.broadcasted_iota(jnp.int32, (8, LANES), 1)
        work = jnp.where(lanes < 8, gram_ref[0] / reps, jnp.where(lanes == rows + 8, 1.0, 0.0))
        for j in range(8):
            root = jnp.sqrt(work[j:j + 1, j:j + 1])
            pivot = work[j:j + 1, :] / root
            below = work[:, j:j + 1] / root
            work = jnp.where(rows == j, pivot, jnp.where(rows > j, work - below * pivot, work))
        inverse[...] = work
        left = left_ref[...]
        total = jnp.zeros_like(left)
        for k in range(8):
            total += work[:, 8 + k:9 + k] * left[k:k + 1, :]
        one, two, three = pieces(total)
        zero = jnp.zeros_like(total)
        basis[...] = jnp.concatenate([one, one, one, two, two, three, zero, zero], axis=0).astype(bf16)

    work = inverse[...]
    right = jnp.concatenate([whole_ref[t] for t in range(whole_ref.shape[0])], axis=1)
    q_new = jnp.zeros_like(right)
    for k in range(8):
        q_new += work[:, 8 + k:9 + k] * right[k:k + 1, :]
    q_new = q_new / reps
    q_ref[...] = q_new
    one, two, three = pieces(q_new)
    zero = jnp.zeros_like(q_new)
    factor = jnp.concatenate([one, two, three, one, two, one, zero, zero], axis=0).astype(bf16)
    taken = lax.dot_general(basis[...], factor, TN, preferred_element_type=f32)
    out_ref[...] = (merged_ref[...] + partner_ref[...].astype(f32) - taken).astype(bf16)


def exchange(x, axes):
    return lax.all_to_all(x, axes, 0, 0)


def body(heads_out, out_grad, drop_mask, timestep, error_old, q_start):
    weighed, heads, error = out_grad[0], heads_out[0], error_old[0]
    tok, dout = weighed.shape
    n_tok, feats = heads.shape
    rank = q_start.shape[1]
    mine = n_tok // 2
    tiles = dout // LANES
    half = lax.axis_index("xh")
    n_seq, n_rep = lax.axis_size(SEQ), lax.axis_size(REP)
    n_pair, n_group = lax.axis_size(PAIR), lax.axis_size(GROUP)
    q_t = q_start.T

    weighted, proj = call(
        weigh_kernel,
        [arr((tok, dout), bf16), arr((n_seq, rank, tok), f32)],
        [SMEM, SMEM, VMEM, VMEM],
        2 * 32 * tok * dout,
        (drop_mask, timestep, weighed, q_t),
    )
    gathered = lax.all_gather(weighted, "y", axis=0, tiled=True)
    away = lax.dynamic_slice_in_dim(heads, (1 - half) * mine, mine, 0)
    here = lax.dynamic_slice_in_dim(heads, half * mine, mine, 0)
    swap = [(0, 1), (1, 0)]
    partner = lax.ppermute(away, "xh", swap)

    (first,) = call(error_left_kernel, [arr((rank, feats), f32)], [VMEM] * 2, 2 * 32 * feats * dout, (q_t, error))
    (parts,) = call(
        left_kernel,
        [arr((n_rep, rank, feats), f32)],
        [VMEM] * 3,
        2 * 32 * n_tok * feats,
        (exchange(proj, SEQ), heads, first),
    )
    left, token = call(
        token_kernel,
        [arr((rank, feats), f32), arr((n_seq, rank, tok), f32)],
        [VMEM] * 2,
        2 * 32 * n_tok * feats,
        (exchange(parts, REP), heads),
    )
    right, gram = call(
        error_right_kernel,
        [arr((rank, dout), f32), arr((rank, LANES), f32)],
        [VMEM] * 2,
        2 * 32 * feats * dout,
        (left, error),
    )
    (pieces_out,) = call(
        right_kernel,
        [arr((n_group, rank, LANES), f32)],
        [VMEM] * 4,
        2 * 32 * tok * dout,
        (exchange(token, SEQ), weighted, right, gram),
    )
    (tile,) = call(sum_kernel, [arr((n_pair, rank, LANES), f32)], [VMEM], n_group * rank * LANES, (exchange(pieces_out, GROUP),))

    gathered, tile, partner = lax.optimization_barrier((gathered, tile, partner))
    other_sum = lax.dot_general(partner, gathered, TN, preferred_element_type=f32).astype(bf16)
    (tile,) = call(sum_kernel, [arr((n_group, rank, LANES), f32)], [VMEM], n_pair * rank * LANES, (exchange(tile, PAIR),))
    tile, other_sum, gathered, here = lax.optimization_barrier((tile, other_sum, gathered, here))
    from_partner = lax.ppermute(other_sum, "xh", swap)
    merged = lax.dot_general(here, gathered, TN, preferred_element_type=f32) + error.astype(f32)
    whole = exchange(tile, GROUP)

    wide = 4
    cols = wide * LANES
    q_new, error_next = pl.pallas_call(
        functools.partial(final_kernel, float(n_rep)),
        grid=(tiles // wide,),
        out_shape=[arr((rank, dout), f32), arr((feats, dout), bf16)],
        in_specs=[
            pl.BlockSpec((1, rank, LANES), lambda i: (tiles, 0, 0)),
            pl.BlockSpec((wide, rank, LANES), lambda i: (i, 0, 0)),
            pl.BlockSpec((rank, feats), lambda i: (0, 0)),
            pl.BlockSpec((feats, cols), lambda i: (0, i)),
            pl.BlockSpec((feats, cols), lambda i: (0, i)),
        ],
        out_specs=[
            pl.BlockSpec((rank, cols), lambda i: (0, i)),
            pl.BlockSpec((feats, cols), lambda i: (0, i)),
        ],
        scratch_shapes=[pltpu.VMEM((8, LANES), f32), pltpu.VMEM((64, feats), bf16)],
        cost_estimate=pl.CostEstimate(flops=2 * 64 * feats * dout, bytes_accessed=8 * feats * dout, transcendentals=0),
    )(whole, whole, left, merged, from_partner)
    return (q_new.T, error_next[None])


def solution(mesh):
    split = Mesh(mesh.devices.reshape(2, 8, 2, 12, 2), SEQ + REP)
    in_specs = (
        P(REP, None, SEQ),
        P(REP, SEQ, None),
        P(REP),
        P(REP),
        P(REP, SEQ, None),
        P(),
    )
    out_specs = (P(), P(REP, SEQ, None))
    return jax.shard_map(body, mesh=split, in_specs=in_specs, out_specs=out_specs, check_vma=False)
```

time: 178 us -> 173 us (0.972)
  Pallas kernels: 0 us -> 22.9 us
  between operations: 26.8 us -> 15.4 us
  matrix products: 19.6 us -> 10.7 us
  other arithmetic: 5.16 us -> 0 us
  starting transfers between devices: 47.4 us -> 52.1 us
  local copies, waits for them, and re-layouts: 7.76 us -> 3.39 us
  blocking collectives: 18.9 us -> 16.2 us
    pallas_call x0 -> x9, Pallas kernels: none -> 22.9 us  [the longest x8 16.9 us: call(): pl.pallas_call(kernel, out_shape=outs, in_specs=ins, out_specs=[VMEM] * l...]
    dot_general x12 -> x2, matrix products: 19.6 us -> 10.7 us  [the longest x1 5.52 us: body(): lax.dot_general(here, gathered, TN, preferred_element_type=f32)]
    all_to_all x5, waiting for transfers between devices: 43 us -> 51.6 us  [exchange(): return lax.all_to_all(x, axes, 0, 0)]
    ppermute x1, waiting for transfers between devices: 7.88 us -> 0.01 us  [body(): from_partner = lax.ppermute(other_sum, 'xh', swap)]
    all_to_all x5, starting transfers between devices: 39.6 us -> 46 us  [exchange(): return lax.all_to_all(x, axes, 0, 0)]
    slice x8 -> x0, local copies, waits for them, and re-layouts: 4.62 us -> none  [body(): pivot = work[j] * lax.rsqrt(work[j, j])]
    unnamed x10 -> x14, local copies, waits for them, and re-layouts: 0.03 us -> 3.31 us
    all_to_all x1, blocking collectives: 18.9 us -> 16.2 us  [exchange(): return lax.all_to_all(x, axes, 0, 0)]
  transfers between devices with their start and end apart: 8 -> 8, of which waited for: 6 -> 5; matrix products, arithmetic and copies ran while one was open for 13% -> 6% of each run, Pallas kernels for 0% -> 8%
where the time goes in v2:
time: 173 us; the launch traced here: 172 us
  starting transfers between devices  52.1 us (30%)
  waiting for transfers between devices  51.6 us (30%)
  Pallas kernels  22.9 us (13%)
  blocking collectives  16.2 us (9%)
  between operations  15.4 us (9%)
  matrix products  10.7 us (6%)
  local copies, waits for them, and re-layouts  3.39 us (2%)
    all_to_all x5, waiting for transfers between devices, exchange(): return lax.all_to_all(x, axes, 0, 0)  51.6 us
    all_to_all x5, starting transfers between devices, exchange(): return lax.all_to_all(x, axes, 0, 0)  46 us
    pallas_call x8, Pallas kernels, call(): pl.pallas_call(kernel, out_shape=outs, in_specs=ins, out_specs=[VMEM] * l...  16.9 us
    all_to_all x1, blocking collectives, exchange(): return lax.all_to_all(x, axes, 0, 0)  16.2 us
    pallas_call x1, Pallas kernels, body(): pl.pallas_call(functools.partial(final_kernel, float(n_rep)), grid=(tiles...  6.09 us
    dot_general x1, matrix products, body(): lax.dot_general(here, gathered, TN, preferred_element_type=f32)  5.52 us
    dot_general x1, matrix products, body(): lax.dot_general(partner, gathered, TN, preferred_element_type=f32)  5.19 us
  transfers between devices with their start and end apart: 8, of which 5 were waited for; matrix products, arithmetic and copies ran while one was open for 6% of the time, Pallas kernels for 8%

profile of v2, /device:TPU:1, one launch (start us, length us, event | category | flops | bytes accessed | tf_op | source)
XLA Modules:
  0.0 172.4 jit_solution(10961298728049892111)
XLA Ops:
  7.2 0.0 all-gather.2.cloned.1.call-start
  8.5 0.0 copy-start.1
  8.5 2.2 %shard_map.77 = (bf16[128,2560]{1,0:T(8,128)(2,1)}, f32[16,8,128]{2,1,0:T(8,128)}) custom-call(s32[1]{0:T(128)S(6)} %copy.8.drop_ref, s32[1]{0:T(128)S(6)} %copy.9.step_ref, bf16[128,2560]{1,0:T(8,128)(2,1)} %bitcast.19, f32[8,2560]{1,0:T(8,128)} %bitcast.20), custom_call_target="tpu_custom_call" | custom-call | flops 20971520 | bytes 1458184 | tf_op jit(solution)/shard_map/pallas_call | solution.py:44
  10.7 0.0 all-gather.2.cloned.1.call-update
  10.7 10.2 %all-to-all-start = ((f32[16,8,128]{2,1,0:T(8,128)}), f32[16,8,128]{2,1,0:T(8,128)S(1)}, u32[]{:S(2)}, u32[]{:S(2)}) async-start(f32[16,8,128]{2,1,0:T(8,128)} %get-tuple-element.18), calls=%async_computation | async-start | bytes 131072 | tf_op jit(solution)/shard_map/all_to_all | solution.py:151
  21.0 2.4 %shard_map.78.first_ref = f32[8,256]{1,0:T(8,128)} custom-call(f32[8,2560]{1,0:T(8,128)} %bitcast.21, bf16[256,2560]{1,0:T(8,128)(2,1)} %bitcast.15), custom_call_target="tpu_custom_call" | custom-call | flops 41943040 | bytes 1400832 | tf_op jit(solution)/shard_map/pallas_call | solution.py:44
  23.4 6.4 %all-to-all-done.proj_ref = f32[16,8,128]{2,1,0:T(8,128)S(1)} async-done(((f32[16,8,128]{2,1,0:T(8,128)}), f32[16,8,128]{2,1,0:T(8,128)S(1)}, u32[]{:S(2)}, u32[]{:S(2)}) %all-to-all-start) | async-done | bytes 65568 | tf_op jit(solution)/shard_map/all_to_all | solution.py:151
  29.8 0.0 copy-start.6
  29.9 0.6 copy-done.6
  30.5 2.3 %shard_map.79 = f32[48,8,256]{2,1,0:T(8,128)} custom-call(f32[16,8,128]{2,1,0:T(8,128)} %copy-done.6, bf16[2048,256]{1,0:T(8,128)(2,1)} %bitcast.17, f32[8,256]{1,0:T(8,128)} %shard_map.78.first_ref), custom_call_target="tpu_custom_call" | custom-call | flops 33554432 | bytes 1515520 | tf_op jit(solution)/shard_map/pallas_call | solution.py:44
  32.8 17.6 %all-to-all-start.1 = ((f32[48,8,256]{2,1,0:T(8,128)}), f32[48,8,256]{2,1,0:T(8,128)S(1)}, u32[]{:S(2)}, u32[]{:S(2)}) async-start(f32[48,8,256]{2,1,0:T(8,128)} %shard_map.79), calls=%async_computation.1 | async-start | bytes 786432 | tf_op jit(solution)/shard_map/all_to_all | solution.py:151
  50.4 0.0 copy-done.1
  50.4 0.1 dynamic-slice_bitcast_fusion
  50.5 3.0 %collective-permute-start = (bf16[1024,256]{1,0:T(8,128)(2,1)S(1)}, bf16[1024,256]{1,0:T(8,128)(2,1)S(1)}, u32[]{:S(2)}, u32[]{:S(2)}) collective-permute-start(bf16[1024,256]{1,0:T(8,128)(2,1)S(1)} %get-tuple-element.33), channel_id=1, source_target_pairs={{0,384},{384,0},{1,385},{385,1},{2,386},{386,2},{3,387},{387,3},{4... | collective-permute-start | bytes 1572872 | tf_op jit(solution)/shard_map/ppermute | solution.py:177
  53.5 14.7 %all-to-all-done.1.parts_ref = f32[48,8,256]{2,1,0:T(8,128)S(1)} async-done(((f32[48,8,256]{2,1,0:T(8,128)}), f32[48,8,256]{2,1,0:T(8,128)S(1)}, u32[]{:S(2)}, u32[]{:S(2)}) %all-to-all-start.1) | async-done | bytes 393248 | tf_op jit(solution)/shard_map/all_to_all | solution.py:151
  68.2 0.0 copy-start.2
  68.2 0.8 copy-done.2
  68.9 2.4 %shard_map.80 = (f32[8,256]{1,0:T(8,128)}, f32[16,8,128]{2,1,0:T(8,128)}) custom-call(f32[48,8,256]{2,1,0:T(8,128)} %copy-done.2, bf16[2048,256]{1,0:T(8,128)(2,1)} %bitcast.18), custom_call_target="tpu_custom_call" | custom-call | flops 33554432 | bytes 1515520 | tf_op jit(solution)/shard_map/pallas_call | solution.py:44
  71.4 3.5 %all-to-all-start.2 = ((f32[16,8,128]{2,1,0:T(8,128)}), f32[16,8,128]{2,1,0:T(8,128)S(1)}, u32[]{:S(2)}, u32[]{:S(2)}) async-start(f32[16,8,128]{2,1,0:T(8,128)} %get-tuple-element.19), calls=%async_computation.2 | async-start | bytes 131072 | tf_op jit(solution)/shard_map/all_to_all | solution.py:151
  74.9 2.3 %shard_map.81 = (f32[8,2560]{1,0:T(8,128)}, f32[8,128]{1,0:T(8,128)}) custom-call(f32[8,256]{1,0:T(8,128)} %get-tuple-element.20.left_ref, bf16[256,2560]{1,0:T(8,128)(2,1)} %bitcast.16), custom_call_target="tpu_custom_call" | custom-call | flops 41943040 | bytes 1404928 | tf_op jit(solution)/shard_map/pallas_call | solution.py:44
  77.2 6.7 %all-to-all-done.2.token_ref = f32[16,8,128]{2,1,0:T(8,128)S(1)} async-done(((f32[16,8,128]{2,1,0:T(8,128)}), f32[16,8,128]{2,1,0:T(8,128)S(1)}, u32[]{:S(2)}, u32[]{:S(2)}) %all-to-all-start.2) | async-done | bytes 65568 | tf_op jit(solution)/shard_map/all_to_all | solution.py:151
  83.9 0.0 copy-start.5
  83.9 0.6 copy-done.5
  84.5 2.0 %shard_map.82 = f32[32,8,128]{2,1,0:T(8,128)} custom-call(f32[16,8,128]{2,1,0:T(8,128)} %copy-done.5, bf16[128,2560]{1,0:T(8,128)(2,1)} %get-tuple-element.17.weighted_ref, f32[8,2560]{1,0:T(8,128)} %get-tuple-element.21.right_ref, f32[8,128]{1,0:T(8,128)} %get-tuple-element.22.gram_ref), custom_call_target="tpu_custom_call" | custom-call | flops 20971520 | bytes 937984 | tf_op jit(solution)/shard_map/pallas_call | solution.py:44
  86.5 16.2 %all_to_all.30.parts_ref = f32[32,8,128]{2,1,0:T(8,128)} all-to-all(f32[32,8,128]{2,1,0:T(8,128)} %shard_map.82), channel_id=1, replica_groups=mesh['xh'=2,'y'=8,'xl'=2,'z'=12,'c'=2] {'xh','y','c'}, dimensions={0} | all-to-all | bytes 262144 | tf_op jit(solution)/shard_map/all_to_all | solution.py:151
  102.7 1.6 shard_map.83
  104.3 0.0 collective-permute-done
  104.3 0.0 all-gather.2.cloned.1.call-done
  104.3 6.7 %all-to-all-start.4 = ((f32[24,8,128]{2,1,0:T(8,128)}), f32[24,8,128]{2,1,0:T(8,128)S(1)}, u32[]{:S(2)}, u32[]{:S(2)}) async-start(f32[24,8,128]{2,1,0:T(8,128)} %shard_map.83), calls=%async_computation.4 | async-start | bytes 196608 | tf_op jit(solution)/shard_map/all_to_all | solution.py:151
  111.1 0.0 copy-start
  111.1 5.2 %convolution_convert_fusion = bf16[256,2560]{1,0:T(8,128)(2,1)} fusion(bf16[1024,256]{1,0:T(8,128)(2,1)S(1)} %collective-permute-done, bf16[1024,2560]{1,0:T(8,128)(2,1)} %all-gather.2.cloned.1.call-done), kind=kOutput, calls=%fused_computation.1 | convolution fusion | flops 1342832640 | bytes 7077888 | tf_op jit(solution)/shard_map/dot_general | solution.py:211
  116.3 4.6 %all-to-all-done.4.parts_ref = f32[24,8,128]{2,1,0:T(8,128)S(1)} async-done(((f32[24,8,128]{2,1,0:T(8,128)}), f32[24,8,128]{2,1,0:T(8,128)S(1)}, u32[]{:S(2)}, u32[]{:S(2)}) %all-to-all-start.4) | async-done | bytes 98336 | tf_op jit(solution)/shard_map/all_to_all | solution.py:151
  120.8 0.0 copy-start.4
  120.8 0.6 copy-done.4
  121.5 1.6 shard_map.84
  123.0 3.0 %collective-permute-start.1 = (bf16[256,2560]{1,0:T(8,128)(2,1)}, bf16[256,2560]{1,0:T(8,128)(2,1)}, u32[]{:S(2)}, u32[]{:S(2)}) collective-permute-start(bf16[256,2560]{1,0:T(8,128)(2,1)} %convolution_convert_fusion), channel_id=1, source_target_pairs={{0,384},{384,0},{1,385},{385,1},{2,386},{386,2},{3,387},{387,3},{4... | collective-permute-start | bytes 3932168 | tf_op jit(solution)/shard_map/ppermute | solution.py:214
  126.1 8.0 %all-to-all-start.5 = ((f32[32,8,128]{2,1,0:T(8,128)}), f32[32,8,128]{2,1,0:T(8,128)S(1)}, u32[]{:S(2)}, u32[]{:S(2)}) async-start(f32[32,8,128]{2,1,0:T(8,128)} %shard_map.84), calls=%async_computation.5 | async-start | bytes 262144 | tf_op jit(solution)/shard_map/all_to_all | solution.py:151
  134.0 0.0 copy-done
  134.0 5.5 %convolution_add_fusion.merged_ref = f32[256,2560]{1,0:T(8,128)} fusion(bf16[1024,256]{1,0:T(8,128)(2,1)S(1)} %get-tuple-element.27, bf16[1024,2560]{1,0:T(8,128)(2,1)} %all-gather.2.cloned.1.call-done, bf16[1,256,2560]{2,1,0:T(8,128)(2,1)S(1)} %copy-done), kind=kOutput, calls=%fused_computation | convolution fusion | flops 1343488000 | bytes 9699328 | tf_op jit(solution)/shard_map/dot_general | solution.py:215
  139.6 19.3 %all-to-all-done.5.gram_ref.whole_ref = f32[32,8,128]{2,1,0:T(8,128)S(1)} async-done(((f32[32,8,128]{2,1,0:T(8,128)}), f32[32,8,128]{2,1,0:T(8,128)S(1)}, u32[]{:S(2)}, u32[]{:S(2)}) %all-to-all-start.5) | async-done | bytes 131104 | tf_op jit(solution)/shard_map/all_to_all | solution.py:151
  158.9 0.0 copy-start.3
  158.9 0.0 collective-permute-done.1.partner_ref
  158.9 0.6 copy-done.3
  159.5 6.1 %shard_map.85 = (f32[8,2560]{1,0:T(8,128)}, bf16[256,2560]{1,0:T(8,128)(2,1)}) custom-call(f32[32,8,128]{2,1,0:T(8,128)} %copy-done.3, f32[32,8,128]{2,1,0:T(8,128)} %copy-done.3, f32[8,256]{1,0:T(8,128)} %get-tuple-element.20.left_ref, f32[256,2560]{1,0:T(8,128)} %convolution_add_fusion.merged_ref, bf16[256,2560]{1,0:T(8,128)(2,1)} %collective-permute-done.1.partner_ref), custom_call_target="tpu_custom_call" | custom-call | flops 83886080 | bytes 5242880 | tf_op jit(solution)/shard_map/pallas_call | solution.py:220
Async XLA Ops:
  7.2 97.2 %all-gather.2.cloned.1.call-start = ((), (), s32[]{:S(2)}) async-start(), calls=%async_computation.6 | async-start | bytes 5898240 | tf_op jit(solution)/shard_map/all_gather | solution.py:173
  8.5 41.9 %copy-start.1 = (bf16[1,2048,256]{2,1,0:T(8,128)(2,1)S(1)}, bf16[1,2048,256]{2,1,0:T(8,128)(2,1)}, u32[]{:S(2)}) copy-start(bf16[1,2048,256]{2,1,0:T(8,128)(2,1)} %param.6) | copy-start | bytes 3145732
  10.7 19.1 %all-to-all-start = ((f32[16,8,128]{2,1,0:T(8,128)}), f32[16,8,128]{2,1,0:T(8,128)S(1)}, u32[]{:S(2)}, u32[]{:S(2)}) async-start(f32[16,8,128]{2,1,0:T(8,128)} %get-tuple-element.18), calls=%async_computation | async-start | bytes 131072 | tf_op jit(solution)/shard_map/all_to_all | solution.py:151
  29.8 0.6 copy-start.6
  32.8 35.4 %all-to-all-start.1 = ((f32[48,8,256]{2,1,0:T(8,128)}), f32[48,8,256]{2,1,0:T(8,128)S(1)}, u32[]{:S(2)}, u32[]{:S(2)}) async-start(f32[48,8,256]{2,1,0:T(8,128)} %shard_map.79), calls=%async_computation.1 | async-start | bytes 786432 | tf_op jit(solution)/shard_map/all_to_all | solution.py:151
  50.5 53.8 %collective-permute-start = (bf16[1024,256]{1,0:T(8,128)(2,1)S(1)}, bf16[1024,256]{1,0:T(8,128)(2,1)S(1)}, u32[]{:S(2)}, u32[]{:S(2)}) collective-permute-start(bf16[1024,256]{1,0:T(8,128)(2,1)S(1)} %get-tuple-element.33), channel_id=1, source_target_pairs={{0,384},{384,0},{1,385},{385,1},{2,386},{386,2},{3,387},{387,3},{4... | collective-permute-start | bytes 1572872 | tf_op jit(solution)/shard_map/ppermute | solution.py:177
  68.2 0.8 copy-start.2
  71.4 12.5 %all-to-all-start.2 = ((f32[16,8,128]{2,1,0:T(8,128)}), f32[16,8,128]{2,1,0:T(8,128)S(1)}, u32[]{:S(2)}, u32[]{:S(2)}) async-start(f32[16,8,128]{2,1,0:T(8,128)} %get-tuple-element.19), calls=%async_computation.2 | async-start | bytes 131072 | tf_op jit(solution)/shard_map/all_to_all | solution.py:151
  83.9 0.6 copy-start.5
  104.3 16.5 %all-to-all-start.4 = ((f32[24,8,128]{2,1,0:T(8,128)}), f32[24,8,128]{2,1,0:T(8,128)S(1)}, u32[]{:S(2)}, u32[]{:S(2)}) async-start(f32[24,8,128]{2,1,0:T(8,128)} %shard_map.83), calls=%async_computation.4 | async-start | bytes 196608 | tf_op jit(solution)/shard_map/all_to_all | solution.py:151
  111.1 22.9 %copy-start = (bf16[1,256,2560]{2,1,0:T(8,128)(2,1)S(1)}, bf16[1,256,2560]{2,1,0:T(8,128)(2,1)}, u32[]{:S(2)}) copy-start(bf16[1,256,2560]{2,1,0:T(8,128)(2,1)} %param.10) | copy-start | bytes 3932164
  120.8 0.6 copy-start.4
  123.0 35.8 %collective-permute-start.1 = (bf16[256,2560]{1,0:T(8,128)(2,1)}, bf16[256,2560]{1,0:T(8,128)(2,1)}, u32[]{:S(2)}, u32[]{:S(2)}) collective-permute-start(bf16[256,2560]{1,0:T(8,128)(2,1)} %convolution_convert_fusion), channel_id=1, source_target_pairs={{0,384},{384,0},{1,385},{385,1},{2,386},{386,2},{3,387},{387,3},{4... | collective-permute-start | bytes 3932168 | tf_op jit(solution)/shard_map/ppermute | solution.py:214
  126.1 32.8 %all-to-all-start.5 = ((f32[32,8,128]{2,1,0:T(8,128)}), f32[32,8,128]{2,1,0:T(8,128)S(1)}, u32[]{:S(2)}, u32[]{:S(2)}) async-start(f32[32,8,128]{2,1,0:T(8,128)} %shard_map.84), calls=%async_computation.5 | async-start | bytes 262144 | tf_op jit(solution)/shard_map/all_to_all | solution.py:151
  158.9 0.7 copy-start.3
Sparse Core Ops, SparseCore 0:
  10.9 78.6 all-gather.1

commit v3 on v1

v3 whole, which is shorter than its diff:
```python
import functools

import jax
import jax.numpy as jnp
from jax import lax
from jax.experimental import pallas as pl
from jax.experimental.pallas import tpu as pltpu
from jax.sharding import Mesh, PartitionSpec as P

STEPS = 1000
PROMPT = 128
SEQ = ("xh", "y")
REP = ("xl", "z", "c")
PAIR = ("z", "c")
GROUP = ("xh", "y", "xl")
LANES = 128
highest = lax.Precision.HIGHEST
f32 = jnp.float32
bf16 = jnp.bfloat16
VMEM = pl.BlockSpec(memory_space=pltpu.VMEM)
SMEM = pl.BlockSpec(memory_space=pltpu.SMEM)
NT = (((1,), (1,)), ((), ()))
TN = (((0,), (0,)), ((), ()))


def pieces(x):
    first = x.astype(bf16).astype(f32)
    rest = x - first
    second = rest.astype(bf16).astype(f32)
    return first, second, rest - second


def stacked(x):
    return jnp.concatenate(pieces(x) + (jnp.zeros_like(x),), axis=0).astype(bf16)


def folded(x):
    return x[0:8] + x[8:16] + x[16:24]


def call(kernel, outs, ins, flops, args, limit=0):
    size = lambda a: a.size * a.dtype.itemsize
    moved = sum(size(a) for a in args) + sum(size(a) for a in outs)
    return pl.pallas_call(
        kernel,
        out_shape=outs,
        in_specs=ins,
        out_specs=[VMEM] * len(outs),
        compiler_params=pltpu.CompilerParams(vmem_limit_bytes=limit) if limit else None,
        cost_estimate=pl.CostEstimate(flops=flops, bytes_accessed=moved, transcendentals=0),
    )(*args)


def arr(shape, dtype):
    return jax.ShapeDtypeStruct(shape, dtype)


def weigh_kernel(drop_ref, step_ref, grad_ref, q_ref, weighted_ref, proj_ref):
    tok = grad_ref.shape[0]
    place = lax.axis_index("xh") * lax.axis_size("y") + lax.axis_index("y")
    position = place * tok + lax.broadcasted_iota(jnp.int32, (tok, 1), 0)
    drop = jnp.full((tok, 1), drop_ref[0], jnp.int32)
    step = jnp.full((tok, 1), step_ref[0], jnp.int32).astype(f32)
    keeping = jnp.logical_or(position >= PROMPT, drop == 1)
    weights = jnp.where(keeping, 0.5 + 1.5 * step / STEPS, 0.0)
    weighted = (grad_ref[...].astype(f32) * weights).astype(bf16)
    weighted_ref[...] = weighted
    proj = folded(lax.dot_general(stacked(q_ref[...]), weighted, NT, preferred_element_type=f32))
    for s in range(proj_ref.shape[0]):
        proj_ref[s] = proj


def factor_kernel(reps, whole_ref, left_ref, q_ref, basis_ref, factor_ref):
    tiles = q_ref.shape[1] // LANES
    rows = lax.broadcasted_iota(jnp.int32, (8, LANES), 0)
    lanes = lax.broadcasted_iota(jnp.int32, (8, LANES), 1)
    work = jnp.where(lanes < 8, whole_ref[tiles] / reps, jnp.where(lanes == rows + 8, 1.0, 0.0))
    for j in range(8):
        column = jnp.broadcast_to(work[:, j:j + 1], (8, LANES))
        scale = 1.0 / jnp.sqrt(column[j:j + 1, :])
        pivot = work[j:j + 1, :] * scale
        work = jnp.where(rows == j, pivot, jnp.where(rows > j, work - column * scale * pivot, work))

    left = left_ref[...]
    right = jnp.concatenate([whole_ref[t] for t in range(tiles)], axis=1)
    basis = jnp.zeros_like(left)
    q_new = jnp.zeros_like(right)
    for k in range(8):
        weight = work[:, 8 + k:9 + k]
        basis += weight * left[k:k + 1, :]
        q_new += weight * right[k:k + 1, :]
    q_new = q_new / reps
    q_ref[...] = q_new
    one, two, three = pieces(basis)
    zero = jnp.zeros_like(basis)
    basis_ref[...] = jnp.concatenate([one, one, one, two, two, three, zero, zero], axis=0).astype(bf16)
    one, two, three = pieces(q_new)
    zero = jnp.zeros_like(q_new)
    factor_ref[...] = jnp.concatenate([one, two, three, one, two, one, zero, zero], axis=0).astype(bf16)


def exchange(x, axes):
    return lax.all_to_all(x, axes, 0, 0)


def spread(x, axes):
    return exchange(jnp.broadcast_to(x[None], (lax.axis_size(axes),) + x.shape), axes)


def body(heads_out, out_grad, drop_mask, timestep, error_old, q_start):
    heads, error = heads_out[0], error_old[0]
    tok, dout = out_grad.shape[1:]
    n_tok, feats = heads.shape
    rank = q_start.shape[1]
    tiles = dout // LANES
    half = lax.axis_index("xh")
    n_seq, n_rep, n_group = lax.axis_size(SEQ), lax.axis_size(REP), lax.axis_size(GROUP)
    q_t = q_start.T
    wide_heads = heads.astype(f32).reshape(n_seq, tok, feats)

    weighted, proj = call(
        weigh_kernel,
        [arr((tok, dout), bf16), arr((n_seq, rank, tok), f32)],
        [SMEM, SMEM, VMEM, VMEM],
        2 * 32 * tok * dout,
        (drop_mask, timestep, out_grad[0], q_t),
    )
    swap = [(0, 1), (1, 0)]
    gathered = lax.all_gather(weighted, "y", axis=0, tiled=True)
    mine = n_tok // lax.axis_size("xh")
    partner = lax.ppermute(lax.dynamic_slice_in_dim(heads, (1 - half) * mine, mine, 0), "xh", swap)
    here = lax.dynamic_slice_in_dim(heads, half * mine, mine, 0)

    first = jnp.einsum("kd,fd->kf", q_t, error.astype(f32), precision=highest)
    proj, first = lax.optimization_barrier((exchange(proj, SEQ), first))
    left_part = jnp.einsum("skt,stf->kf", proj, wide_heads, precision=highest) + first
    left = jnp.sum(spread(left_part, REP), axis=0)
    token_part = jnp.einsum("kf,stf->skt", left, wide_heads, precision=highest)
    right_error = jnp.dot(left, error.astype(f32), precision=highest)
    gram_part = jnp.dot(left, left.T, precision=highest)
    token, right_error, gram_part = lax.optimization_barrier((exchange(token_part, SEQ), right_error, gram_part))
    token = jnp.sum(token, axis=0)
    right_part = jnp.dot(token, weighted.astype(f32), precision=highest) + right_error
    parts = right_part.reshape(rank, tiles, LANES).transpose(1, 0, 2)
    gram_tile = jnp.pad(gram_part, ((0, 0), (0, LANES - rank)))[None]
    parts = jnp.concatenate([parts, gram_tile, jnp.zeros((n_group - tiles - 1, rank, LANES), f32)], axis=0)
    other_sum = lax.dot_general(partner, gathered, TN, preferred_element_type=f32).astype(bf16)
    parts, other_sum = lax.optimization_barrier((exchange(parts, GROUP), other_sum))
    tile = jnp.sum(parts, axis=0)
    from_partner = lax.ppermute(other_sum, "xh", swap)
    tile = jnp.sum(spread(tile, PAIR), axis=0)
    own_sum = lax.dot_general(here, gathered, TN, preferred_element_type=f32) + error.astype(f32)
    whole, own_sum = lax.optimization_barrier((spread(tile, GROUP), own_sum))
    q_new, basis, factor = call(
        functools.partial(factor_kernel, float(n_rep)),
        [arr((rank, dout), f32), arr((8 * rank, feats), bf16), arr((8 * rank, dout), bf16)],
        [VMEM] * 2,
        100 * rank * dout,
        (whole, left),
        8 << 20,
    )
    taken = lax.dot_general(basis, factor, TN, preferred_element_type=f32)
    error_next = (own_sum + from_partner.astype(f32) - taken).astype(bf16)
    return (q_new.T, error_next[None])


def solution(mesh):
    split = Mesh(mesh.devices.reshape(2, 8, 2, 12, 2), SEQ + REP)
    in_specs = (
        P(REP, None, SEQ),
        P(REP, SEQ, None),
        P(REP),
        P(REP),
        P(REP, SEQ, None),
        P(),
    )
    out_specs = (P(), P(REP, SEQ, None))
    return jax.shard_map(body, mesh=split, in_specs=in_specs, out_specs=out_specs, check_vma=False)
```

time: 178 us -> 154 us (0.87)
  blocking collectives: 18.9 us -> 0 us
  starting transfers between devices: 47.4 us -> 61.1 us
  between operations: 26.8 us -> 15.5 us
  local copies, waits for them, and re-layouts: 7.76 us -> 3.07 us
  Pallas kernels: 0 us -> 3.57 us
  matrix products: 19.6 us -> 16.9 us
  waiting for transfers between devices: 50.9 us -> 48.8 us
    all_to_all x1 -> x0, blocking collectives: 18.9 us -> none  [spread(): return lax.all_to_all(jnp.broadcast_to(x[None], (n,) + x.shape), axes, 0, 0)]
    all_to_all x5 -> x6, starting transfers between devices: 39.6 us -> 54.5 us  [exchange(): return lax.all_to_all(x, axes, 0, 0)]
    ppermute x1, waiting for transfers between devices: 7.88 us -> 0.01 us  [body(): from_partner = lax.ppermute(other_sum, 'xh', swap)]
    slice x8 -> x0, local copies, waits for them, and re-layouts: 4.62 us -> none  [body(): pivot = work[j] * lax.rsqrt(work[j, j])]
    all_gather x1, waiting for transfers between devices: 0.02 us -> 3.86 us  [body(): gathered = lax.all_gather(weighted, 'y', axis=0, tiled=True)]
    pallas_call x0 -> x2, Pallas kernels: none -> 3.57 us  [call(): pl.pallas_call(kernel, out_shape=outs, in_specs=ins, out_specs=[VMEM] * l...]
    broadcast_in_dim x8 -> x1, other arithmetic: 0.04 us -> 3 us  [body(): return (q_new.T, error_next[None])]
    dot_general x11 -> x8, matrix products: 19.5 us -> 16.8 us  [the longest x1 5.53 us: body(): lax.dot_general(here, gathered, TN, preferred_element_type=f32)]
  transfers between devices with their start and end apart: 8 -> 9, of which waited for: 6 -> 7; matrix products, arithmetic and copies ran while one was open for 13% -> 14% of each run, Pallas kernels for 0% -> 1%
where the time goes in v3:
time: 154 us; the launch traced here: 153 us
  starting transfers between devices  61.1 us (40%)
  waiting for transfers between devices  48.8 us (32%)
  matrix products  16.9 us (11%)
  between operations  15.5 us (10%)
  other arithmetic  3.89 us (3%)
  Pallas kernels  3.57 us (2%)
  local copies, waits for them, and re-layouts  3.07 us (2%)
    all_to_all x6, starting transfers between devices, exchange(): return lax.all_to_all(x, axes, 0, 0)  54.5 us
    all_to_all x6, waiting for transfers between devices, exchange(): return lax.all_to_all(x, axes, 0, 0)  44.9 us
    dot_general x1, matrix products, body(): lax.dot_general(here, gathered, TN, preferred_element_type=f32)  5.53 us
    dot_general x1, matrix products, body(): lax.dot_general(partner, gathered, TN, preferred_element_type=f32)  5.26 us
    all_gather x1, waiting for transfers between devices, body(): gathered = lax.all_gather(weighted, 'y', axis=0, tiled=True)  3.86 us
    ppermute x1, starting transfers between devices, body(): from_partner = lax.ppermute(other_sum, 'xh', swap)  3.77 us
    pallas_call x2, Pallas kernels, call(): pl.pallas_call(kernel, out_shape=outs, in_specs=ins, out_specs=[VMEM] * l...  3.57 us
  transfers between devices with their start and end apart: 9, of which 7 were waited for; matrix products, arithmetic and copies ran while one was open for 14% of the time, Pallas kernels for 1%

profile of v3, /device:TPU:1, one launch (start us, length us, event | category | flops | bytes accessed | tf_op | source)
XLA Modules:
  0.0 152.9 jit_solution(9419059598097747036)
XLA Ops:
  7.2 0.0 copy-start
  7.2 0.0 all-gather.2.cloned.1.call-start
  8.6 2.1 %shard_map.77 = (bf16[128,2560]{1,0:T(8,128)(2,1)}, f32[16,8,128]{2,1,0:T(8,128)}) custom-call(s32[1]{0:T(128)S(6)} %copy.8.drop_ref, s32[1]{0:T(128)S(6)} %copy.9.step_ref, bf16[128,2560]{1,0:T(8,128)(2,1)} %bitcast.48, f32[8,2560]{1,0:T(8,128)} %bitcast.49), custom_call_target="tpu_custom_call" | custom-call | flops 20971520 | bytes 1458184 | tf_op jit(solution)/shard_map/pallas_call | solution.py:44
  10.7 0.0 all-gather.2.cloned.1.call-update
  10.7 10.2 %all-to-all-start = ((f32[16,8,128]{2,1,0:T(8,128)}), f32[16,8,128]{2,1,0:T(8,128)S(1)}, u32[]{:S(2)}, u32[]{:S(2)}) async-start(f32[16,8,128]{2,1,0:T(8,128)} %get-tuple-element.16), calls=%async_computation | async-start | bytes 131072 | tf_op jit(solution)/shard_map/all_to_all | solution.py:103
  21.0 2.5 %fusion.3 = f32[8,256]{1,0:T(8,128)S(1)} fusion(f32[2560,8]{0,1:T(8,128)} %param.11, bf16[1,256,2560]{2,1,0:T(8,128)(2,1)} %param.10), kind=kOutput, calls=%fused_computation.7 | convolution fusion | flops 62914560 | bytes 1400832 | tf_op jit(solution)/shard_map/kd,fd->kf/dot_general | solution.py:134
  23.4 0.0 copy-start.1
  23.4 6.4 %all-to-all-done = f32[16,8,128]{2,1,0:T(8,128)S(1)} async-done(((f32[16,8,128]{2,1,0:T(8,128)}), f32[16,8,128]{2,1,0:T(8,128)S(1)}, u32[]{:S(2)}, u32[]{:S(2)}) %all-to-all-start) | async-done | bytes 65568 | tf_op jit(solution)/shard_map/all_to_all | solution.py:103
  29.8 0.0 copy-done
  29.8 0.5 fusion.6
  30.4 0.0 copy-start.3
  30.4 0.8 broadcast_in_dim.12
  31.2 17.6 %all-to-all-start.1 = ((f32[48,8,256]{2,1,0:T(8,128)}), f32[48,8,256]{2,1,0:T(8,128)S(1)}, u32[]{:S(2)}, u32[]{:S(2)}) async-start(f32[48,8,256]{2,1,0:T(8,128)} %broadcast_in_dim.12), calls=%async_computation.1 | async-start | bytes 786432 | tf_op jit(solution)/shard_map/all_to_all | solution.py:103
  48.8 0.9 dynamic-slice_bitcast_fusion
  49.7 2.9 %collective-permute-start = (bf16[1024,256]{1,0:T(8,128)(2,1)}, bf16[1024,256]{1,0:T(8,128)(2,1)}, u32[]{:S(2)}, u32[]{:S(2)}) collective-permute-start(bf16[1024,256]{1,0:T(8,128)(2,1)} %dynamic-slice_bitcast_fusion), channel_id=1, source_target_pairs={{0,384},{384,0},{1,385},{385,1},{2,386},{386,2},{3,387},{387,3},{4... | collective-permute-start | bytes 1572872 | tf_op jit(solution)/shard_map/ppermute | solution.py:131
  52.6 0.1 pad.7.clone
  52.6 13.9 %all-to-all-done.1 = f32[48,8,256]{2,1,0:T(8,128)S(1)} async-done(((f32[48,8,256]{2,1,0:T(8,128)}), f32[48,8,256]{2,1,0:T(8,128)S(1)}, u32[]{:S(2)}, u32[]{:S(2)}) %all-to-all-start.1) | async-done | bytes 393248 | tf_op jit(solution)/shard_map/all_to_all | solution.py:103
  66.6 0.1 reduce_sum.36.left_ref
  66.6 1.6 %convolution_bitcast_fusion = f32[16,8,128]{2,1,0:T(8,128)} fusion(bf16[16,128,256]{2,1,0:T(8,128)(2,1)S(1)} %bitcast.47, f32[8,256]{1,0:T(8,128)S(1)} %reduce_sum.36.left_ref), kind=kOutput, calls=%fused_computation.10 | convolution fusion | flops 50331648 | bytes 1122304 | tf_op jit(solution)/shard_map/kf,stf->skt/dot_general | solution.py:138
  68.2 3.5 %all-to-all-start.2 = ((f32[16,8,128]{2,1,0:T(8,128)}), f32[16,8,128]{2,1,0:T(8,128)S(1)}, u32[]{:S(2)}, u32[]{:S(2)}) async-start(f32[16,8,128]{2,1,0:T(8,128)} %convolution_bitcast_fusion), calls=%async_computation.2 | async-start | bytes 131072 | tf_op jit(solution)/shard_map/all_to_all | solution.py:103
  71.7 0.0 copy-done.1
  71.7 0.6 fusion.1
  72.3 0.1 fusion.11
  72.4 8.2 %all-to-all-done.2 = f32[16,8,128]{2,1,0:T(8,128)S(1)} async-done(((f32[16,8,128]{2,1,0:T(8,128)}), f32[16,8,128]{2,1,0:T(8,128)S(1)}, u32[]{:S(2)}, u32[]{:S(2)}) %all-to-all-start.2) | async-done | bytes 65568 | tf_op jit(solution)/shard_map/all_to_all | solution.py:103
  80.7 0.0 copy-done.3
  80.7 0.4 fusion.5
  81.1 0.8 maximum_maximum_fusion
  81.8 4.0 %all-to-all-start.3 = ((f32[32,8,128]{2,1,0:T(8,128)}), f32[32,8,128]{2,1,0:T(8,128)S(1)}, u32[]{:S(2)}, u32[]{:S(2)}) async-start(f32[32,8,128]{2,1,0:T(8,128)} %maximum_maximum_fusion), calls=%async_computation.3 | async-start | bytes 262144 | tf_op jit(solution)/shard_map/all_to_all | solution.py:103
  85.8 0.0 collective-permute-done
  85.8 3.9 %all-gather.2.cloned.1.call-done = bf16[1024,2560]{1,0:T(8,128)(2,1)} async-done(((bf16[128,2560]{1,0:T(8,128)(2,1)}), bf16[1024,2560]{1,0:T(8,128)(2,1)}) %all-gather.2.cloned.1.call-update) | async-done | bytes 5242896 | tf_op jit(solution)/shard_map/all_gather | solution.py:129
  89.7 5.3 %convolution_convert_fusion = bf16[256,2560]{1,0:T(8,128)(2,1)} fusion(bf16[1024,256]{1,0:T(8,128)(2,1)} %collective-permute-done, bf16[1024,2560]{1,0:T(8,128)(2,1)} %all-gather.2.cloned.1.call-done), kind=kOutput, calls=%fused_computation.1 | convolution fusion | flops 1342832640 | bytes 7077888 | tf_op jit(solution)/shard_map/dot_general | solution.py:147
  94.9 0.8 all-to-all-done.3
  95.8 3.8 %collective-permute-start.1 = (bf16[256,2560]{1,0:T(8,128)(2,1)}, bf16[256,2560]{1,0:T(8,128)(2,1)}, u32[]{:S(2)}, u32[]{:S(2)}) collective-permute-start(bf16[256,2560]{1,0:T(8,128)(2,1)} %convolution_convert_fusion), channel_id=1, source_target_pairs={{0,384},{384,0},{1,385},{385,1},{2,386},{386,2},{3,387},{387,3},{4... | collective-permute-start | bytes 3932168 | tf_op jit(solution)/shard_map/ppermute | solution.py:150
  99.6 0.6 broadcast_in_dim.30
  100.2 13.9 %all-to-all-start.4 = ((f32[24,8,128]{2,1,0:T(8,128)}), f32[24,8,128]{2,1,0:T(8,128)S(1)}, u32[]{:S(2)}, u32[]{:S(2)}) async-start(f32[24,8,128]{2,1,0:T(8,128)} %broadcast_in_dim.30), calls=%async_computation.4 | async-start | bytes 196608 | tf_op jit(solution)/shard_map/all_to_all | solution.py:103
  114.1 11.1 %all-to-all-done.4 = f32[24,8,128]{2,1,0:T(8,128)S(1)} async-done(((f32[24,8,128]{2,1,0:T(8,128)}), f32[24,8,128]{2,1,0:T(8,128)S(1)}, u32[]{:S(2)}, u32[]{:S(2)}) %all-to-all-start.4) | async-done | bytes 98336 | tf_op jit(solution)/shard_map/all_to_all | solution.py:103
  125.2 0.7 broadcast_in_dim.31
  125.8 5.3 %all-to-all-start.5 = ((f32[32,8,128]{2,1,0:T(8,128)}), f32[32,8,128]{2,1,0:T(8,128)S(1)}, u32[]{:S(2)}, u32[]{:S(2)}) async-start(f32[32,8,128]{2,1,0:T(8,128)} %broadcast_in_dim.31), calls=%async_computation.5 | async-start | bytes 262144 | tf_op jit(solution)/shard_map/all_to_all | solution.py:103
  131.1 5.5 %convolution_add_fusion = f32[256,2560]{1,0:T(8,128)} fusion(bf16[1024,2560]{1,0:T(8,128)(2,1)} %all-gather.2.cloned.1.call-done, bf16[1,256,2560]{2,1,0:T(8,128)(2,1)S(1)} %copy-done.1, bf16[1,2048,256]{2,1,0:T(8,128)(2,1)S(1)} %copy-done, s32[]{:T(128)S(6)} %select_n.7), kind=kOutput, calls=%fused_computation | convolution fusion | flops 1343488000 | bytes 9699332 | tf_op jit(solution)/shard_map/dot_general | solution.py:152
  136.6 4.4 %all-to-all-done.5.whole_ref = f32[32,8,128]{2,1,0:T(8,128)S(1)} async-done(((f32[32,8,128]{2,1,0:T(8,128)}), f32[32,8,128]{2,1,0:T(8,128)S(1)}, u32[]{:S(2)}, u32[]{:S(2)}) %all-to-all-start.5) | async-done | bytes 131104 | tf_op jit(solution)/shard_map/all_to_all | solution.py:103
  141.1 0.0 copy-start.2
  141.1 1.5 shard_map.78
  142.5 0.5 fusion.12
  143.1 0.0 collective-permute-done.1
  143.1 0.0 copy-done.2
  143.1 3.0 %fusion = bf16[1,256,2560]{2,1,0:T(8,128)(2,1)} fusion(f32[256,2560]{1,0:T(8,128)S(1)} %fusion.12, f32[256,2560]{1,0:T(8,128)S(1)} %copy-done.2, bf16[256,2560]{1,0:T(8,128)(2,1)} %collective-permute-done.1), kind=kLoop, calls=%fused_computation.4 | loop fusion | flops 2621440 | bytes 7864320 | tf_op jit(solution)/shard_map/broadcast_in_dim | solution.py:164
  (5 shorter events, 0.1 us)
Async XLA Ops:
  7.2 22.7 %copy-start = (bf16[1,2048,256]{2,1,0:T(8,128)(2,1)S(1)}, bf16[1,2048,256]{2,1,0:T(8,128)(2,1)}, u32[]{:S(2)}) copy-start(bf16[1,2048,256]{2,1,0:T(8,128)(2,1)} %param.6) | copy-start | bytes 3145732
  7.2 82.5 %all-gather.2.cloned.1.call-start = ((), (), s32[]{:S(2)}) async-start(), calls=%async_computation.6 | async-start | bytes 5898240 | tf_op jit(solution)/shard_map/all_gather | solution.py:129
  10.7 19.1 %all-to-all-start = ((f32[16,8,128]{2,1,0:T(8,128)}), f32[16,8,128]{2,1,0:T(8,128)S(1)}, u32[]{:S(2)}, u32[]{:S(2)}) async-start(f32[16,8,128]{2,1,0:T(8,128)} %get-tuple-element.16), calls=%async_computation | async-start | bytes 131072 | tf_op jit(solution)/shard_map/all_to_all | solution.py:103
  23.4 48.3 %copy-start.1 = (bf16[1,256,2560]{2,1,0:T(8,128)(2,1)S(1)}, bf16[1,256,2560]{2,1,0:T(8,128)(2,1)}, u32[]{:S(2)}) copy-start(bf16[1,256,2560]{2,1,0:T(8,128)(2,1)} %param.10) | copy-start | bytes 3932164
  30.4 50.3 %copy-start.3 = (bf16[128,2560]{1,0:T(8,128)(2,1)S(1)}, bf16[128,2560]{1,0:T(8,128)(2,1)}, u32[]{:S(2)}) copy-start(bf16[128,2560]{1,0:T(8,128)(2,1)} %get-tuple-element.20) | copy-start | bytes 1966084
  31.2 35.4 %all-to-all-start.1 = ((f32[48,8,256]{2,1,0:T(8,128)}), f32[48,8,256]{2,1,0:T(8,128)S(1)}, u32[]{:S(2)}, u32[]{:S(2)}) async-start(f32[48,8,256]{2,1,0:T(8,128)} %broadcast_in_dim.12), calls=%async_computation.1 | async-start | bytes 786432 | tf_op jit(solution)/shard_map/all_to_all | solution.py:103
  49.7 36.1 %collective-permute-start = (bf16[1024,256]{1,0:T(8,128)(2,1)}, bf16[1024,256]{1,0:T(8,128)(2,1)}, u32[]{:S(2)}, u32[]{:S(2)}) collective-permute-start(bf16[1024,256]{1,0:T(8,128)(2,1)} %dynamic-slice_bitcast_fusion), channel_id=1, source_target_pairs={{0,384},{384,0},{1,385},{385,1},{2,386},{386,2},{3,387},{387,3},{4... | collective-permute-start | bytes 1572872 | tf_op jit(solution)/shard_map/ppermute | solution.py:131
  68.2 12.5 %all-to-all-start.2 = ((f32[16,8,128]{2,1,0:T(8,128)}), f32[16,8,128]{2,1,0:T(8,128)S(1)}, u32[]{:S(2)}, u32[]{:S(2)}) async-start(f32[16,8,128]{2,1,0:T(8,128)} %convolution_bitcast_fusion), calls=%async_computation.2 | async-start | bytes 131072 | tf_op jit(solution)/shard_map/all_to_all | solution.py:103
  81.8 13.9 %all-to-all-start.3 = ((f32[32,8,128]{2,1,0:T(8,128)}), f32[32,8,128]{2,1,0:T(8,128)S(1)}, u32[]{:S(2)}, u32[]{:S(2)}) async-start(f32[32,8,128]{2,1,0:T(8,128)} %maximum_maximum_fusion), calls=%async_computation.3 | async-start | bytes 262144 | tf_op jit(solution)/shard_map/all_to_all | solution.py:103
  95.8 47.3 %collective-permute-start.1 = (bf16[256,2560]{1,0:T(8,128)(2,1)}, bf16[256,2560]{1,0:T(8,128)(2,1)}, u32[]{:S(2)}, u32[]{:S(2)}) collective-permute-start(bf16[256,2560]{1,0:T(8,128)(2,1)} %convolution_convert_fusion), channel_id=1, source_target_pairs={{0,384},{384,0},{1,385},{385,1},{2,386},{386,2},{3,387},{387,3},{4... | collective-permute-start | bytes 3932168 | tf_op jit(solution)/shard_map/ppermute | solution.py:150
  100.2 24.9 %all-to-all-start.4 = ((f32[24,8,128]{2,1,0:T(8,128)}), f32[24,8,128]{2,1,0:T(8,128)S(1)}, u32[]{:S(2)}, u32[]{:S(2)}) async-start(f32[24,8,128]{2,1,0:T(8,128)} %broadcast_in_dim.30), calls=%async_computation.4 | async-start | bytes 196608 | tf_op jit(solution)/shard_map/all_to_all | solution.py:103
  125.8 15.2 %all-to-all-start.5 = ((f32[32,8,128]{2,1,0:T(8,128)}), f32[32,8,128]{2,1,0:T(8,128)S(1)}, u32[]{:S(2)}, u32[]{:S(2)}) async-start(f32[32,8,128]{2,1,0:T(8,128)} %broadcast_in_dim.31), calls=%async_computation.5 | async-start | bytes 262144 | tf_op jit(solution)/shard_map/all_to_all | solution.py:103
  141.1 2.0 %copy-start.2 = (f32[256,2560]{1,0:T(8,128)S(1)}, f32[256,2560]{1,0:T(8,128)}, u32[]{:S(2)}) copy-start(f32[256,2560]{1,0:T(8,128)} %convolution_add_fusion) | copy-start | bytes 7864324
Sparse Core Ops, SparseCore 0:
  11.0 78.6 all-gather.1

commit v4 on v3

--- a/solution.py
+++ b/solution.py
@@ -55,7 +55,7 @@
     return jax.ShapeDtypeStruct(shape, dtype)
 
 
-def weigh_kernel(drop_ref, step_ref, grad_ref, q_ref, weighted_ref, proj_ref):
+def weigh_kernel(drop_ref, step_ref, grad_ref, q_ref, weighted_ref, keep_ref, send_ref, proj_ref):
     tok = grad_ref.shape[0]
     place = lax.axis_index("xh") * lax.axis_size("y") + lax.axis_index("y")
     position = place * tok + lax.broadcasted_iota(jnp.int32, (tok, 1), 0)
@@ -65,6 +65,19 @@
     weights = jnp.where(keeping, 0.5 + 1.5 * step / STEPS, 0.0)
     weighted = (grad_ref[...].astype(f32) * weights).astype(bf16)
     weighted_ref[...] = weighted
+    cut = keep_ref.shape[1]
+    low, high = weighted[:, :cut], weighted[:, cut:]
+
+    @pl.when(lax.axis_index("xh") == 0)
+    def _():
+        keep_ref[...] = low
+        send_ref[...] = high
+
+    @pl.when(lax.axis_index("xh") == 1)
+    def _():
+        keep_ref[...] = high
+        send_ref[...] = low
+
     proj = folded(lax.dot_general(stacked(q_ref[...]), weighted, NT, preferred_element_type=f32))
     for s in range(proj_ref.shape[0]):
         proj_ref[s] = proj
@@ -118,23 +131,36 @@
     q_t = q_start.T
     wide_heads = heads.astype(f32).reshape(n_seq, tok, feats)
 
-    weighted, proj = call(
+    weighted, keep, send, proj = call(
         weigh_kernel,
-        [arr((tok, dout), bf16), arr((n_seq, rank, tok), f32)],
+        [arr((tok, dout), bf16), arr((tok, dout // 2), bf16), arr((tok, dout // 2), bf16), arr((n_seq, rank, tok), f32)],
         [SMEM, SMEM, VMEM, VMEM],
         2 * 32 * tok * dout,
         (drop_mask, timestep, out_grad[0], q_t),
     )
     swap = [(0, 1), (1, 0)]
-    gathered = lax.all_gather(weighted, "y", axis=0, tiled=True)
-    mine = n_tok // lax.axis_size("xh")
-    partner = lax.ppermute(lax.dynamic_slice_in_dim(heads, (1 - half) * mine, mine, 0), "xh", swap)
-    here = lax.dynamic_slice_in_dim(heads, half * mine, mine, 0)
-
+    received = lax.ppermute(send, "xh", swap)
+    low = half == 0
+    rows = jnp.concatenate([jnp.where(low, keep, received), jnp.where(low, received, keep)], axis=0)
     first = jnp.einsum("kd,fd->kf", q_t, error.astype(f32), precision=highest)
-    proj, first = lax.optimization_barrier((exchange(proj, SEQ), first))
+    proj, rows, first = lax.optimization_barrier((exchange(proj, SEQ), rows, first))
+    gathered = lax.all_gather(rows, "y", axis=0, tiled=True)
+    halves = lax.axis_size("xh")
+    own = heads.reshape(halves, n_seq // halves, tok, feats).transpose(1, 0, 2, 3).reshape(n_tok, feats)
+    own = lax.optimization_barrier(own)
+    early, late = jnp.split(own, 2)
+    early = lax.ppermute(early, "xh", swap)
+
     left_part = jnp.einsum("skt,stf->kf", proj, wide_heads, precision=highest) + first
-    left = jnp.sum(spread(left_part, REP), axis=0)
+    cores = lax.axis_size("c")
+    share = feats // cores
+    left_part = lax.psum(left_part, "c")
+    left_part = lax.dynamic_slice_in_dim(left_part, lax.axis_index("c") * share, share, 1)
+    left = jnp.sum(spread(left_part, REP).reshape(n_rep // cores, cores, rank, share), axis=0)
+    left = jnp.concatenate([left[i] for i in range(cores)], axis=1)
+    late, _ = lax.optimization_barrier((late, left))
+    late = lax.ppermute(late, "xh", swap)
+    partner = jnp.concatenate([early, late], axis=0)
     token_part = jnp.einsum("kf,stf->skt", left, wide_heads, precision=highest)
     right_error = jnp.dot(left, error.astype(f32), precision=highest)
     gram_part = jnp.dot(left, left.T, precision=highest)
@@ -144,12 +170,12 @@
     parts = right_part.reshape(rank, tiles, LANES).transpose(1, 0, 2)
     gram_tile = jnp.pad(gram_part, ((0, 0), (0, LANES - rank)))[None]
     parts = jnp.concatenate([parts, gram_tile, jnp.zeros((n_group - tiles - 1, rank, LANES), f32)], axis=0)
+    tile = jnp.sum(exchange(parts, GROUP), axis=0)
     other_sum = lax.dot_general(partner, gathered, TN, preferred_element_type=f32).astype(bf16)
-    parts, other_sum = lax.optimization_barrier((exchange(parts, GROUP), other_sum))
+    from_partner = lax.ppermute(other_sum, "xh", swap)
+    parts, _ = lax.optimization_barrier((spread(tile, PAIR), other_sum))
     tile = jnp.sum(parts, axis=0)
-    from_partner = lax.ppermute(other_sum, "xh", swap)
-    tile = jnp.sum(spread(tile, PAIR), axis=0)
-    own_sum = lax.dot_general(here, gathered, TN, preferred_element_type=f32) + error.astype(f32)
+    own_sum = lax.dot_general(own, gathered, TN, preferred_element_type=f32)
     whole, own_sum = lax.optimization_barrier((spread(tile, GROUP), own_sum))
     q_new, basis, factor = call(
         functools.partial(factor_kernel, float(n_rep)),
@@ -160,7 +186,14 @@
         8 << 20,
     )
     taken = lax.dot_general(basis, factor, TN, preferred_element_type=f32)
-    error_next = (own_sum + from_partner.astype(f32) - taken).astype(bf16)
+    cut = dout // 2
+    far = from_partner.astype(f32)
+    sums = [jnp.where(low, own_sum, far), jnp.where(low, far, own_sum)]
+    error_next = [
+        (sums[i] + error[:, i * cut:(i + 1) * cut].astype(f32) - taken[:, i * cut:(i + 1) * cut]).astype(bf16)
+        for i in range(2)
+    ]
+    error_next = jnp.concatenate(error_next, axis=1)
     return (q_new.T, error_next[None])
 
 

time: 154 us -> 150 us (0.974)
  blocking collectives: 0 us -> 25.5 us
  waiting for transfers between devices: 48.8 us -> 24.5 us
  starting transfers between devices: 61.1 us -> 50 us
  other arithmetic: 3.89 us -> 6.21 us
  local copies, waits for them, and re-layouts: 3.07 us -> 5.31 us
  matrix products: 16.9 us -> 18.6 us
    all_to_all x6 -> x5, waiting for transfers between devices: 44.9 us -> 24.5 us  [exchange(): return lax.all_to_all(x, axes, 0, 0)]
    all_to_all x6 -> x5, starting transfers between devices: 54.5 us -> 34.5 us  [exchange(): return lax.all_to_all(x, axes, 0, 0)]
    all_to_all x0 -> x1, blocking collectives: none -> 17.2 us  [exchange(): return lax.all_to_all(x, axes, 0, 0)]
    ppermute x1 -> x3, starting transfers between devices: 2.89 us -> 13.1 us  [the longest x1 5.6 us: body(): received = lax.ppermute(send, 'xh', swap)]
    psum x0 -> x1, blocking collectives: none -> 8.22 us  [body(): left_part = lax.psum(left_part, 'c')]
    all_gather x1, waiting for transfers between devices: 3.86 us -> 0.02 us  [body(): gathered = lax.all_gather(rows, 'y', axis=0, tiled=True)]
    broadcast_in_dim x1, other arithmetic: 3 us -> 1.14 us  [body(): return (q_new.T, error_next[None])]
  transfers between devices with their start and end apart: 9 -> 10, of which waited for: 7 -> 5; matrix products, arithmetic and copies ran while one was open for 14% -> 18% of each run, Pallas kernels for 1% -> 1%
where the time goes in v4:
time: 150 us; the launch traced here: 149 us
  starting transfers between devices  50 us (33%)
  blocking collectives  25.5 us (17%)
  waiting for transfers between devices  24.5 us (16%)
  matrix products  18.6 us (12%)
  between operations  15.5 us (10%)
  other arithmetic  6.21 us (4%)
  local copies, waits for them, and re-layouts  5.31 us (4%)
  Pallas kernels  3.84 us (3%)
    all_to_all x5, starting transfers between devices, exchange(): return lax.all_to_all(x, axes, 0, 0)  34.5 us
    all_to_all x5, waiting for transfers between devices, exchange(): return lax.all_to_all(x, axes, 0, 0)  24.5 us
    all_to_all x1, blocking collectives, exchange(): return lax.all_to_all(x, axes, 0, 0)  17.2 us
    psum x1, blocking collectives, body(): left_part = lax.psum(left_part, 'c')  8.22 us
    ppermute x1, starting transfers between devices, body(): received = lax.ppermute(send, 'xh', swap)  5.6 us
    dot_general x1, matrix products, body(): lax.dot_general(partner, gathered, TN, preferred_element_type=f32)  5.25 us
    dot_general x1, matrix products, body(): own_sum = lax.dot_general(own, gathered, TN, preferred_element_type=f32)  5.1 us
    ppermute x1, starting transfers between devices, body(): late = lax.ppermute(late, 'xh', swap)  4.63 us
  transfers between devices with their start and end apart: 10, of which 5 were waited for; matrix products, arithmetic and copies ran while one was open for 18% of the time, Pallas kernels for 1%

profile of v4, /device:TPU:1, one launch (start us, length us, event | category | flops | bytes accessed | tf_op | source)
XLA Modules:
  0.0 149.5 jit_solution(2489954309847504931)
XLA Ops:
  8.5 2.4 %shard_map.77 = (bf16[128,2560]{1,0:T(8,128)(2,1)}, bf16[128,1280]{1,0:T(8,128)(2,1)}, bf16[128,1280]{1,0:T(8,128)(2,1)}, f32[16,8,128]{2,1,0:T(8,128)}) custom-call(s32[1]{0:T(128)S(6)} %copy.15.drop_ref, s32[1]{0:T(128)S(6)} %copy.16.step_ref, bf16[128,2560]{1,0:T(8,128)(2,1)} %bitcast.54, f32[8,2560]{1,0:T(8,128)} %bitcast.55), custom_call_target="tpu_custom_call" | custom-call | flops 20971520 | bytes 2113544 | tf_op jit(solution)/shard_map/pallas_call | solution.py:44
  10.8 0.0 copy-start.5
  10.8 5.6 %collective-permute-start = (bf16[128,1280]{1,0:T(8,128)(2,1)}, bf16[128,1280]{1,0:T(8,128)(2,1)S(1)}, u32[]{:S(2)}, u32[]{:S(2)}) collective-permute-start(bf16[128,1280]{1,0:T(8,128)(2,1)} %get-tuple-element.21), channel_id=1, source_target_pairs={{0,384},{384,0},{1,385},{385,1},{2,386},{386,2},{3,387},{387,3},{4... | collective-permute-start | bytes 983048 | tf_op jit(solution)/shard_map/ppermute | solution.py:142
  16.4 6.9 %all-to-all-start = ((f32[16,8,128]{2,1,0:T(8,128)}), f32[16,8,128]{2,1,0:T(8,128)S(1)}, u32[]{:S(2)}, u32[]{:S(2)}) async-start(f32[16,8,128]{2,1,0:T(8,128)} %get-tuple-element.19), calls=%async_computation | async-start | bytes 131072 | tf_op jit(solution)/shard_map/all_to_all | solution.py:116
  23.4 0.0 all-gather.2.cloned.1.call-start
  23.5 2.5 %fusion.15 = f32[8,256]{1,0:T(8,128)S(1)} fusion(f32[2560,8]{0,1:T(8,128)} %param.11, bf16[1,256,2560]{2,1,0:T(8,128)(2,1)} %param.10), kind=kOutput, calls=%fused_computation.32 | convolution fusion | flops 62914560 | bytes 1400832 | tf_op jit(solution)/shard_map/kd,fd->kf/dot_general | solution.py:145
  25.9 0.0 collective-permute-done
  25.9 0.0 copy-done.5
  26.0 0.0 copy-start.1
  26.0 0.9 pad_maximum_fusion
  26.9 5.3 %all-to-all-done = f32[16,8,128]{2,1,0:T(8,128)S(1)} async-done(((f32[16,8,128]{2,1,0:T(8,128)}), f32[16,8,128]{2,1,0:T(8,128)S(1)}, u32[]{:S(2)}, u32[]{:S(2)}) %all-to-all-start) | async-done | bytes 65568 | tf_op jit(solution)/shard_map/all_to_all | solution.py:116
  32.3 0.0 all-gather.2.cloned.1.call-update
  32.3 0.0 copy-done.1
  32.3 0.5 fusion.7
  32.8 8.2 %psum.7 = f32[8,256]{1,0:T(8,128)S(1)} all-reduce(f32[8,256]{1,0:T(8,128)S(1)} %fusion.7), channel_id=1, replica_groups=mesh['xh'=2,'y'=8,'xl'=2,'z'=12,'c'=2] {'c'}, use_global_device_ids=true, to_apply=%region_0.1 | all-reduce | flops 2048 | bytes 16384 | tf_op jit(solution)/shard_map/psum | solution.py:157
  41.1 0.7 broadcast_in_dim.12
  41.8 13.1 %all-to-all-start.1 = ((f32[48,8,128]{2,1,0:T(8,128)}), f32[48,8,128]{2,1,0:T(8,128)}, u32[]{:S(2)}, u32[]{:S(2)}) async-start(f32[48,8,128]{2,1,0:T(8,128)} %broadcast_in_dim.12), calls=%async_computation.1 | async-start | bytes 393216 | tf_op jit(solution)/shard_map/all_to_all | solution.py:116
  54.9 0.1 copy.12
  55.0 0.0 copy-start
  55.0 1.0 fusion.18
  56.0 2.9 %collective-permute-start.1 = (bf16[1024,256]{1,0:T(8,128)(2,1)}, bf16[1024,256]{1,0:T(8,128)(2,1)}, u32[]{:S(2)}, u32[]{:S(2)}) collective-permute-start(bf16[1024,256]{1,0:T(8,128)(2,1)} %get-tuple-element.38), channel_id=1, source_target_pairs={{0,384},{384,0},{1,385},{385,1},{2,386},{386,2},{3,387},{387,3},{4... | collective-permute-start | bytes 1572872 | tf_op jit(solution)/shard_map/ppermute | solution.py:152
  58.9 0.6 pad.11.clone
  59.6 8.4 %all-to-all-done.1 = f32[48,8,128]{2,1,0:T(8,128)} async-done(((f32[48,8,128]{2,1,0:T(8,128)}), f32[48,8,128]{2,1,0:T(8,128)}, u32[]{:S(2)}, u32[]{:S(2)}) %all-to-all-start.1) | async-done | bytes 196640 | tf_op jit(solution)/shard_map/all_to_all | solution.py:116
  68.0 1.0 reduce_sum.36
  69.0 1.5 %convolution_bitcast_fusion.1 = f32[16,8,128]{2,1,0:T(8,128)} fusion(bf16[16,128,256]{2,1,0:T(8,128)(2,1)S(1)} %bitcast.51, f32[8,128]{1,0:T(8,128)S(1)} %get-tuple-element.43, f32[8,128]{1,0:T(8,128)S(1)} %get-tuple-element.42), kind=kOutput, calls=%fused_computation.13 | convolution fusion | flops 50333696 | bytes 1122304 | tf_op jit(solution)/shard_map/kf,stf->skt/dot_general | solution.py:164
  70.5 0.0 copy-start.4
  70.5 0.0 copy-start.3
  70.5 4.3 %all-to-all-start.2 = ((f32[16,8,128]{2,1,0:T(8,128)}), f32[16,8,128]{2,1,0:T(8,128)}, u32[]{:S(2)}, u32[]{:S(2)}) async-start(f32[16,8,128]{2,1,0:T(8,128)} %convolution_bitcast_fusion.1), calls=%async_computation.2 | async-start | bytes 131072 | tf_op jit(solution)/shard_map/all_to_all | solution.py:116
  74.8 0.0 copy-done
  74.8 1.3 fusion.13
  76.1 0.0 copy-done.4
  76.1 4.6 %collective-permute-start.2 = (bf16[1024,256]{1,0:T(8,128)(2,1)S(1)}, bf16[1024,256]{1,0:T(8,128)(2,1)}, u32[]{:S(2)}, u32[]{:S(2)}) collective-permute-start(bf16[1024,256]{1,0:T(8,128)(2,1)S(1)} %copy-done.4), channel_id=1, source_target_pairs={{0,384},{384,0},{1,385},{385,1},{2,386},{386,2},{3,387},{387,3},{4... | collective-permute-start | bytes 1572872 | tf_op jit(solution)/shard_map/ppermute | solution.py:162
  80.7 0.7 fusion.17
  81.4 2.4 %all-to-all-done.2 = f32[16,8,128]{2,1,0:T(8,128)} async-done(((f32[16,8,128]{2,1,0:T(8,128)}), f32[16,8,128]{2,1,0:T(8,128)}, u32[]{:S(2)}, u32[]{:S(2)}) %all-to-all-start.2) | async-done | bytes 65568 | tf_op jit(solution)/shard_map/all_to_all | solution.py:116
  83.8 0.9 reduce_sum.37
  84.7 0.0 copy-done.3
  84.7 1.2 fusion.6
  85.9 0.7 pad_bitcast_fusion
  86.6 0.7 maximum_maximum_fusion
  87.3 17.2 %all_to_all.30 = f32[32,8,128]{2,1,0:T(8,128)S(1)} all-to-all(f32[32,8,128]{2,1,0:T(8,128)S(1)} %maximum_maximum_fusion), channel_id=1, replica_groups=mesh['xh'=2,'y'=8,'xl'=2,'z'=12,'c'=2] {'xh','y','xl'}, dimensions={0} | all-to-all | bytes 262144 | tf_op jit(solution)/shard_map/all_to_all | solution.py:116
  104.6 0.7 broadcast_in_dim.30
  105.3 6.3 %all-to-all-start.4 = ((f32[24,8,128]{2,1,0:T(8,128)}), f32[24,8,128]{2,1,0:T(8,128)}, u32[]{:S(2)}, u32[]{:S(2)}) async-start(f32[24,8,128]{2,1,0:T(8,128)} %broadcast_in_dim.30), calls=%async_computation.4 | async-start | bytes 196608 | tf_op jit(solution)/shard_map/all_to_all | solution.py:116
  111.6 0.0 collective-permute-done.1
  111.6 0.0 collective-permute-done.2
  111.6 0.0 all-gather.2.cloned.1.call-done
  111.7 5.2 %convolution_convert_fusion = bf16[256,1280]{1,0:T(8,128)(2,1)} fusion(bf16[2048,1280]{1,0:T(8,128)(2,1)} %all-gather.2.cloned.1.call-done, bf16[1024,256]{1,0:T(8,128)(2,1)} %collective-permute-done.2, bf16[1024,256]{1,0:T(8,128)(2,1)} %collective-permute-done.1), kind=kOutput, calls=%fused_computation.2 | convolution fusion | flops 1344602112 | bytes 6946816 | tf_op jit(solution)/shard_map/dot_general | solution.py:174
  116.9 2.3 %collective-permute-start.3 = (bf16[256,1280]{1,0:T(8,128)(2,1)}, bf16[256,1280]{1,0:T(8,128)(2,1)S(1)}, u32[]{:S(2)}, u32[]{:S(2)}) collective-permute-start(bf16[256,1280]{1,0:T(8,128)(2,1)} %convolution_convert_fusion), channel_id=1, source_target_pairs={{0,384},{384,0},{1,385},{385,1},{2,386},{386,2},{3,387},{387,3},{4... | collective-permute-start | bytes 1966088 | tf_op jit(solution)/shard_map/ppermute | solution.py:175
  119.2 3.5 %all-to-all-done.4 = f32[24,8,128]{2,1,0:T(8,128)} async-done(((f32[24,8,128]{2,1,0:T(8,128)}), f32[24,8,128]{2,1,0:T(8,128)}, u32[]{:S(2)}, u32[]{:S(2)}) %all-to-all-start.4) | async-done | bytes 98336 | tf_op jit(solution)/shard_map/all_to_all | solution.py:116
  122.8 0.9 reduce_sum.39
  123.7 0.7 broadcast_in_dim.31
  124.3 3.8 %all-to-all-start.5 = ((f32[32,8,128]{2,1,0:T(8,128)}), f32[32,8,128]{2,1,0:T(8,128)S(1)}, u32[]{:S(2)}, u32[]{:S(2)}) async-start(f32[32,8,128]{2,1,0:T(8,128)} %broadcast_in_dim.31), calls=%async_computation.5 | async-start | bytes 262144 | tf_op jit(solution)/shard_map/all_to_all | solution.py:116
  128.2 5.1 %convolution_bitcast_fusion = f32[256,1280]{1,0:T(8,128)} fusion(bf16[2048,1280]{1,0:T(8,128)(2,1)} %all-gather.2.cloned.1.call-done, bf16[2048,256]{1,0:T(8,128)(2,1)S(1)} %bitcast.53), kind=kOutput, calls=%fused_computation.1 | convolution fusion | flops 1342177280 | bytes 7602176 | tf_op jit(solution)/shard_map/dot_general | solution.py:178
  133.3 4.8 %all-to-all-done.5.whole_ref = f32[32,8,128]{2,1,0:T(8,128)S(1)} async-done(((f32[32,8,128]{2,1,0:T(8,128)}), f32[32,8,128]{2,1,0:T(8,128)S(1)}, u32[]{:S(2)}, u32[]{:S(2)}) %all-to-all-start.5) | async-done | bytes 131104 | tf_op jit(solution)/shard_map/all_to_all | solution.py:116
  138.1 1.5 shard_map.78
  139.6 0.0 copy-start.2
  139.6 0.5 fusion.19
  140.1 0.0 collective-permute-done.3
  140.1 0.8 copy-done.2
  140.9 0.6 fusion.2
  141.5 1.1 maximum_bitcast_fusion
  (6 shorter events, 0.1 us)
Async XLA Ops:
  10.8 15.1 %copy-start.5 = (bf16[128,1280]{1,0:T(8,128)(2,1)S(1)}, bf16[128,1280]{1,0:T(8,128)(2,1)}, u32[]{:S(2)}) copy-start(bf16[128,1280]{1,0:T(8,128)(2,1)} %get-tuple-element.20) | copy-start | bytes 983044
  10.8 15.1 %collective-permute-start = (bf16[128,1280]{1,0:T(8,128)(2,1)}, bf16[128,1280]{1,0:T(8,128)(2,1)S(1)}, u32[]{:S(2)}, u32[]{:S(2)}) collective-permute-start(bf16[128,1280]{1,0:T(8,128)(2,1)} %get-tuple-element.21), channel_id=1, source_target_pairs={{0,384},{384,0},{1,385},{385,1},{2,386},{386,2},{3,387},{387,3},{4... | collective-permute-start | bytes 983048 | tf_op jit(solution)/shard_map/ppermute | solution.py:142
  16.4 15.8 %all-to-all-start = ((f32[16,8,128]{2,1,0:T(8,128)}), f32[16,8,128]{2,1,0:T(8,128)S(1)}, u32[]{:S(2)}, u32[]{:S(2)}) async-start(f32[16,8,128]{2,1,0:T(8,128)} %get-tuple-element.19), calls=%async_computation | async-start | bytes 131072 | tf_op jit(solution)/shard_map/all_to_all | solution.py:116
  23.4 88.3 %all-gather.2.cloned.1.call-start = ((), (), s32[]{:S(2)}) async-start(), calls=%async_computation.6 | async-start | bytes 5898240 | tf_op jit(solution)/shard_map/all_gather | solution.py:147
  26.0 6.3 %copy-start.1 = (bf16[1,2048,256]{2,1,0:T(8,128)(2,1)S(1)}, bf16[1,2048,256]{2,1,0:T(8,128)(2,1)}, u32[]{:S(2)}) copy-start(bf16[1,2048,256]{2,1,0:T(8,128)(2,1)} %param.6) | copy-start | bytes 3145732
  41.8 26.2 %all-to-all-start.1 = ((f32[48,8,128]{2,1,0:T(8,128)}), f32[48,8,128]{2,1,0:T(8,128)}, u32[]{:S(2)}, u32[]{:S(2)}) async-start(f32[48,8,128]{2,1,0:T(8,128)} %broadcast_in_dim.12), calls=%async_computation.1 | async-start | bytes 393216 | tf_op jit(solution)/shard_map/all_to_all | solution.py:116
  55.0 19.8 %copy-start = (bf16[1,256,2560]{2,1,0:T(8,128)(2,1)S(1)}, bf16[1,256,2560]{2,1,0:T(8,128)(2,1)}, u32[]{:S(2)}) copy-start(bf16[1,256,2560]{2,1,0:T(8,128)(2,1)} %param.10) | copy-start | bytes 3932164
  56.0 55.6 %collective-permute-start.1 = (bf16[1024,256]{1,0:T(8,128)(2,1)}, bf16[1024,256]{1,0:T(8,128)(2,1)}, u32[]{:S(2)}, u32[]{:S(2)}) collective-permute-start(bf16[1024,256]{1,0:T(8,128)(2,1)} %get-tuple-element.38), channel_id=1, source_target_pairs={{0,384},{384,0},{1,385},{385,1},{2,386},{386,2},{3,387},{387,3},{4... | collective-permute-start | bytes 1572872 | tf_op jit(solution)/shard_map/ppermute | solution.py:152
  70.5 5.6 %copy-start.4 = (bf16[1024,256]{1,0:T(8,128)(2,1)S(1)}, bf16[1024,256]{1,0:T(8,128)(2,1)}, u32[]{:S(2)}) copy-start(bf16[1024,256]{1,0:T(8,128)(2,1)} %get-tuple-element.28) | copy-start | bytes 1572868
  70.5 14.2 %copy-start.3 = (bf16[128,2560]{1,0:T(8,128)(2,1)S(1)}, bf16[128,2560]{1,0:T(8,128)(2,1)}, u32[]{:S(2)}) copy-start(bf16[128,2560]{1,0:T(8,128)(2,1)} %get-tuple-element.25) | copy-start | bytes 1966084
  70.5 13.3 %all-to-all-start.2 = ((f32[16,8,128]{2,1,0:T(8,128)}), f32[16,8,128]{2,1,0:T(8,128)}, u32[]{:S(2)}, u32[]{:S(2)}) async-start(f32[16,8,128]{2,1,0:T(8,128)} %convolution_bitcast_fusion.1), calls=%async_computation.2 | async-start | bytes 131072 | tf_op jit(solution)/shard_map/all_to_all | solution.py:116
  76.1 35.6 %collective-permute-start.2 = (bf16[1024,256]{1,0:T(8,128)(2,1)S(1)}, bf16[1024,256]{1,0:T(8,128)(2,1)}, u32[]{:S(2)}, u32[]{:S(2)}) collective-permute-start(bf16[1024,256]{1,0:T(8,128)(2,1)S(1)} %copy-done.4), channel_id=1, source_target_pairs={{0,384},{384,0},{1,385},{385,1},{2,386},{386,2},{3,387},{387,3},{4... | collective-permute-start | bytes 1572872 | tf_op jit(solution)/shard_map/ppermute | solution.py:162
  105.3 17.5 %all-to-all-start.4 = ((f32[24,8,128]{2,1,0:T(8,128)}), f32[24,8,128]{2,1,0:T(8,128)}, u32[]{:S(2)}, u32[]{:S(2)}) async-start(f32[24,8,128]{2,1,0:T(8,128)} %broadcast_in_dim.30), calls=%async_computation.4 | async-start | bytes 196608 | tf_op jit(solution)/shard_map/all_to_all | solution.py:116
  116.9 23.2 %collective-permute-start.3 = (bf16[256,1280]{1,0:T(8,128)(2,1)}, bf16[256,1280]{1,0:T(8,128)(2,1)S(1)}, u32[]{:S(2)}, u32[]{:S(2)}) collective-permute-start(bf16[256,1280]{1,0:T(8,128)(2,1)} %convolution_convert_fusion), channel_id=1, source_target_pairs={{0,384},{384,0},{1,385},{385,1},{2,386},{386,2},{3,387},{387,3},{4... | collective-permute-start | bytes 1966088 | tf_op jit(solution)/shard_map/ppermute | solution.py:175
  124.3 13.8 %all-to-all-start.5 = ((f32[32,8,128]{2,1,0:T(8,128)}), f32[32,8,128]{2,1,0:T(8,128)S(1)}, u32[]{:S(2)}, u32[]{:S(2)}) async-start(f32[32,8,128]{2,1,0:T(8,128)} %broadcast_in_dim.31), calls=%async_computation.5 | async-start | bytes 262144 | tf_op jit(solution)/shard_map/all_to_all | solution.py:116
  139.6 1.3 copy-start.2
Sparse Core Ops, SparseCore 0:
  32.4 76.3 all-gather.1

commit v5 on v4

--- a/solution.py
+++ b/solution.py
@@ -55,7 +55,7 @@
     return jax.ShapeDtypeStruct(shape, dtype)
 
 
-def weigh_kernel(drop_ref, step_ref, grad_ref, q_ref, weighted_ref, keep_ref, send_ref, proj_ref):
+def weigh_kernel(drop_ref, step_ref, grad_ref, q_ref, weighted_ref, keep_ref, send_ref, proj_ref, split_ref):
     tok = grad_ref.shape[0]
     place = lax.axis_index("xh") * lax.axis_size("y") + lax.axis_index("y")
     position = place * tok + lax.broadcasted_iota(jnp.int32, (tok, 1), 0)
@@ -78,7 +78,8 @@
         keep_ref[...] = high
         send_ref[...] = low
 
-    proj = folded(lax.dot_general(stacked(q_ref[...]), weighted, NT, preferred_element_type=f32))
+    split_ref[...] = stacked(q_ref[...])
+    proj = folded(lax.dot_general(split_ref[...], weighted, NT, preferred_element_type=f32))
     for s in range(proj_ref.shape[0]):
         proj_ref[s] = proj
 
@@ -131,9 +132,9 @@
     q_t = q_start.T
     wide_heads = heads.astype(f32).reshape(n_seq, tok, feats)
 
-    weighted, keep, send, proj = call(
+    weighted, keep, send, proj, q_split = call(
         weigh_kernel,
-        [arr((tok, dout), bf16), arr((tok, dout // 2), bf16), arr((tok, dout // 2), bf16), arr((n_seq, rank, tok), f32)],
+        [arr((tok, dout), bf16), arr((tok, dout // 2), bf16), arr((tok, dout // 2), bf16), arr((n_seq, rank, tok), f32), arr((4 * rank, dout), bf16)],
         [SMEM, SMEM, VMEM, VMEM],
         2 * 32 * tok * dout,
         (drop_mask, timestep, out_grad[0], q_t),
@@ -142,7 +143,7 @@
     received = lax.ppermute(send, "xh", swap)
     low = half == 0
     rows = jnp.concatenate([jnp.where(low, keep, received), jnp.where(low, received, keep)], axis=0)
-    first = jnp.einsum("kd,fd->kf", q_t, error.astype(f32), precision=highest)
+    first = folded(lax.dot_general(q_split, error, NT, preferred_element_type=f32))
     proj, rows, first = lax.optimization_barrier((exchange(proj, SEQ), rows, first))
     gathered = lax.all_gather(rows, "y", axis=0, tiled=True)
     halves = lax.axis_size("xh")

time: 150 us -> 157 us (1.047)
  starting transfers between devices: 50 us -> 63.2 us
  waiting for transfers between devices: 24.5 us -> 20.4 us
  blocking collectives: 25.5 us -> 23.1 us
    all_to_all x5, starting transfers between devices: 34.5 us -> 46.3 us  [exchange(): return lax.all_to_all(x, axes, 0, 0)]
    all_to_all x5, waiting for transfers between devices: 24.5 us -> 17 us  [exchange(): return lax.all_to_all(x, axes, 0, 0)]
    ppermute x1, waiting for transfers between devices: 0.01 us -> 3.44 us  [body(): received = lax.ppermute(send, 'xh', swap)]
    ppermute x1, starting transfers between devices: 2.89 us -> 5.02 us  [body(): early = lax.ppermute(early, 'xh', swap)]
  transfers between devices with their start and end apart: 10 -> 10, of which waited for: 5 -> 5; matrix products, arithmetic and copies ran while one was open for 18% -> 17% of each run, Pallas kernels for 1% -> 1%
where the time goes in v5:
time: 157 us; the launch traced here: 156 us
  starting transfers between devices  63.2 us (40%)
  blocking collectives  23.1 us (15%)
  waiting for transfers between devices  20.4 us (13%)
  matrix products  18 us (11%)
  between operations  15.5 us (10%)
  other arithmetic  6.24 us (4%)
  local copies, waits for them, and re-layouts  5.79 us (4%)
  Pallas kernels  3.89 us (2%)
    all_to_all x5, starting transfers between devices, exchange(): return lax.all_to_all(x, axes, 0, 0)  46.3 us
    all_to_all x5, waiting for transfers between devices, exchange(): return lax.all_to_all(x, axes, 0, 0)  17 us
    all_to_all x1, blocking collectives, exchange(): return lax.all_to_all(x, axes, 0, 0)  16.4 us
    psum x1, blocking collectives, body(): left_part = lax.psum(left_part, 'c')  6.72 us
    dot_general x1, matrix products, body(): lax.dot_general(partner, gathered, TN, preferred_element_type=f32)  5.25 us
    dot_general x1, matrix products, body(): own_sum = lax.dot_general(own, gathered, TN, preferred_element_type=f32)  5.1 us
    ppermute x1, starting transfers between devices, body(): early = lax.ppermute(early, 'xh', swap)  5.02 us
    ppermute x1, starting transfers between devices, body(): received = lax.ppermute(send, 'xh', swap)  4.78 us
  transfers between devices with their start and end apart: 10, of which 5 were waited for; matrix products, arithmetic and copies ran while one was open for 17% of the time, Pallas kernels for 1%

profile of v5, /device:TPU:1, one launch (start us, length us, event | category | flops | bytes accessed | tf_op | source)
XLA Modules:
  0.0 156.2 jit_solution(9249091285462830675)
XLA Ops:
  8.5 2.4 %shard_map.77 = (bf16[128,2560]{1,0:T(8,128)(2,1)}, bf16[128,1280]{1,0:T(8,128)(2,1)}, bf16[128,1280]{1,0:T(8,128)(2,1)}, f32[16,8,128]{2,1,0:T(8,128)}, bf16[32,2560]{1,0:T(8,128)(2,1)}) custom-call(s32[1]{0:T(128)S(6)} %copy.15.drop_ref, s32[1]{0:T(128)S(6)} %copy.16.step_ref, bf16[128,2560]{1,0:T(8,128)(2,1)} %bitcast.54, f32[8,2560]{1,0:T(8,128)} %bitcast.55), custom_call_target="tpu_custom_call" | custom-call | flops 20971520 | bytes 2277384 | tf_op jit(solution)/shard_map/pallas_call | solution.py:44
  10.9 0.0 copy-start.5
  10.9 10.3 %all-to-all-start = ((f32[16,8,128]{2,1,0:T(8,128)}), f32[16,8,128]{2,1,0:T(8,128)S(1)}, u32[]{:S(2)}, u32[]{:S(2)}) async-start(f32[16,8,128]{2,1,0:T(8,128)} %get-tuple-element.20), calls=%async_computation | async-start | bytes 131072 | tf_op jit(solution)/shard_map/all_to_all | solution.py:117
  21.3 0.0 all-gather.2.cloned.1.call-start
  21.3 4.8 %collective-permute-start = (bf16[128,1280]{1,0:T(8,128)(2,1)}, bf16[128,1280]{1,0:T(8,128)(2,1)S(1)}, u32[]{:S(2)}, u32[]{:S(2)}) collective-permute-start(bf16[128,1280]{1,0:T(8,128)(2,1)} %get-tuple-element.22), channel_id=1, source_target_pairs={{0,384},{384,0},{1,385},{385,1},{2,386},{386,2},{3,387},{387,3},{4... | collective-permute-start | bytes 983048 | tf_op jit(solution)/shard_map/ppermute | solution.py:143
  26.1 1.9 %fusion.15 = f32[32,256]{1,0:T(8,128)S(1)} fusion(bf16[32,2560]{1,0:T(8,128)(2,1)} %get-tuple-element.23, bf16[1,256,2560]{2,1,0:T(8,128)(2,1)} %param.10), kind=kOutput, calls=%fused_computation.34 | convolution fusion | flops 41943040 | bytes 1507328 | tf_op jit(solution)/shard_map/dot_general | solution.py:146
  28.0 3.4 %collective-permute-done = bf16[128,1280]{1,0:T(8,128)(2,1)S(1)} collective-permute-done((bf16[128,1280]{1,0:T(8,128)(2,1)}, bf16[128,1280]{1,0:T(8,128)(2,1)S(1)}, u32[]{:S(2)}, u32[]{:S(2)}) %collective-permute-start) | collective-permute-done | bytes 327712 | tf_op jit(solution)/shard_map/ppermute | solution.py:143
  31.4 0.0 copy-done.5
  31.5 0.0 copy-start.1
  31.5 0.9 pad_maximum_fusion
  32.4 0.0 all-to-all-done
  32.4 0.0 all-gather.2.cloned.1.call-update
  32.4 0.5 copy-done.1
  33.0 0.5 fusion.7
  33.5 6.7 %psum.7 = f32[8,256]{1,0:T(8,128)S(1)} all-reduce(f32[8,256]{1,0:T(8,128)S(1)} %fusion.7), channel_id=1, replica_groups=mesh['xh'=2,'y'=8,'xl'=2,'z'=12,'c'=2] {'c'}, use_global_device_ids=true, to_apply=%region_0.1 | all-reduce | flops 2048 | bytes 16384 | tf_op jit(solution)/shard_map/psum | solution.py:158
  40.2 0.7 broadcast_in_dim.12
  40.9 15.5 %all-to-all-start.1 = ((f32[48,8,128]{2,1,0:T(8,128)}), f32[48,8,128]{2,1,0:T(8,128)}, u32[]{:S(2)}, u32[]{:S(2)}) async-start(f32[48,8,128]{2,1,0:T(8,128)} %broadcast_in_dim.12), calls=%async_computation.1 | async-start | bytes 393216 | tf_op jit(solution)/shard_map/all_to_all | solution.py:117
  56.4 0.1 copy.12
  56.5 0.0 copy-start
  56.5 1.0 fusion.18
  57.6 5.0 %collective-permute-start.1 = (bf16[1024,256]{1,0:T(8,128)(2,1)}, bf16[1024,256]{1,0:T(8,128)(2,1)}, u32[]{:S(2)}, u32[]{:S(2)}) collective-permute-start(bf16[1024,256]{1,0:T(8,128)(2,1)} %get-tuple-element.40), channel_id=1, source_target_pairs={{0,384},{384,0},{1,385},{385,1},{2,386},{386,2},{3,387},{387,3},{4... | collective-permute-start | bytes 1572872 | tf_op jit(solution)/shard_map/ppermute | solution.py:153
  62.6 0.6 pad.11.clone
  63.2 6.3 %all-to-all-done.1 = f32[48,8,128]{2,1,0:T(8,128)} async-done(((f32[48,8,128]{2,1,0:T(8,128)}), f32[48,8,128]{2,1,0:T(8,128)}, u32[]{:S(2)}, u32[]{:S(2)}) %all-to-all-start.1) | async-done | bytes 196640 | tf_op jit(solution)/shard_map/all_to_all | solution.py:117
  69.5 1.0 reduce_sum.36
  70.5 1.5 convolution_bitcast_fusion.1
  72.1 0.0 copy-start.4
  72.1 0.0 copy-start.3
  72.1 9.3 %all-to-all-start.2 = ((f32[16,8,128]{2,1,0:T(8,128)}), f32[16,8,128]{2,1,0:T(8,128)}, u32[]{:S(2)}, u32[]{:S(2)}) async-start(f32[16,8,128]{2,1,0:T(8,128)} %convolution_bitcast_fusion.1), calls=%async_computation.2 | async-start | bytes 131072 | tf_op jit(solution)/shard_map/all_to_all | solution.py:117
  81.4 0.0 copy-done
  81.4 1.3 fusion.13
  82.7 0.0 copy-done.4
  82.7 4.7 %collective-permute-start.2 = (bf16[1024,256]{1,0:T(8,128)(2,1)S(1)}, bf16[1024,256]{1,0:T(8,128)(2,1)}, u32[]{:S(2)}, u32[]{:S(2)}) collective-permute-start(bf16[1024,256]{1,0:T(8,128)(2,1)S(1)} %copy-done.4), channel_id=1, source_target_pairs={{0,384},{384,0},{1,385},{385,1},{2,386},{386,2},{3,387},{387,3},{4... | collective-permute-start | bytes 1572872 | tf_op jit(solution)/shard_map/ppermute | solution.py:163
  87.4 0.7 fusion.17
  88.1 2.3 %all-to-all-done.2 = f32[16,8,128]{2,1,0:T(8,128)} async-done(((f32[16,8,128]{2,1,0:T(8,128)}), f32[16,8,128]{2,1,0:T(8,128)}, u32[]{:S(2)}, u32[]{:S(2)}) %all-to-all-start.2) | async-done | bytes 65568 | tf_op jit(solution)/shard_map/all_to_all | solution.py:117
  90.4 0.9 reduce_sum.37
  91.3 0.0 copy-done.3
  91.3 1.2 fusion.6
  92.5 0.7 pad_bitcast_fusion
  93.2 0.7 maximum_maximum_fusion
  94.0 16.4 %all_to_all.30 = f32[32,8,128]{2,1,0:T(8,128)S(1)} all-to-all(f32[32,8,128]{2,1,0:T(8,128)S(1)} %maximum_maximum_fusion), channel_id=1, replica_groups=mesh['xh'=2,'y'=8,'xl'=2,'z'=12,'c'=2] {'xh','y','xl'}, dimensions={0} | all-to-all | bytes 262144 | tf_op jit(solution)/shard_map/all_to_all | solution.py:117
  110.4 0.7 broadcast_in_dim.30
  111.0 7.3 %all-to-all-start.4 = ((f32[24,8,128]{2,1,0:T(8,128)}), f32[24,8,128]{2,1,0:T(8,128)}, u32[]{:S(2)}, u32[]{:S(2)}) async-start(f32[24,8,128]{2,1,0:T(8,128)} %broadcast_in_dim.30), calls=%async_computation.4 | async-start | bytes 196608 | tf_op jit(solution)/shard_map/all_to_all | solution.py:117
  118.3 0.0 collective-permute-done.1
  118.3 0.0 collective-permute-done.2
  118.3 0.0 all-gather.2.cloned.1.call-done
  118.3 5.2 %convolution_convert_fusion = bf16[256,1280]{1,0:T(8,128)(2,1)} fusion(bf16[2048,1280]{1,0:T(8,128)(2,1)} %all-gather.2.cloned.1.call-done, bf16[1024,256]{1,0:T(8,128)(2,1)} %collective-permute-done.2, bf16[1024,256]{1,0:T(8,128)(2,1)} %collective-permute-done.1), kind=kOutput, calls=%fused_computation.2 | convolution fusion | flops 1344602112 | bytes 6946816 | tf_op jit(solution)/shard_map/dot_general | solution.py:175
  123.6 2.3 %collective-permute-start.3 = (bf16[256,1280]{1,0:T(8,128)(2,1)}, bf16[256,1280]{1,0:T(8,128)(2,1)S(1)}, u32[]{:S(2)}, u32[]{:S(2)}) collective-permute-start(bf16[256,1280]{1,0:T(8,128)(2,1)} %convolution_convert_fusion), channel_id=1, source_target_pairs={{0,384},{384,0},{1,385},{385,1},{2,386},{386,2},{3,387},{387,3},{4... | collective-permute-start | bytes 1966088 | tf_op jit(solution)/shard_map/ppermute | solution.py:176
  125.9 3.5 %all-to-all-done.4 = f32[24,8,128]{2,1,0:T(8,128)} async-done(((f32[24,8,128]{2,1,0:T(8,128)}), f32[24,8,128]{2,1,0:T(8,128)}, u32[]{:S(2)}, u32[]{:S(2)}) %all-to-all-start.4) | async-done | bytes 98336 | tf_op jit(solution)/shard_map/all_to_all | solution.py:117
  129.4 0.9 reduce_sum.39
  130.3 0.7 broadcast_in_dim.31
  131.0 3.8 %all-to-all-start.5 = ((f32[32,8,128]{2,1,0:T(8,128)}), f32[32,8,128]{2,1,0:T(8,128)S(1)}, u32[]{:S(2)}, u32[]{:S(2)}) async-start(f32[32,8,128]{2,1,0:T(8,128)} %broadcast_in_dim.31), calls=%async_computation.5 | async-start | bytes 262144 | tf_op jit(solution)/shard_map/all_to_all | solution.py:117
  134.9 5.1 %convolution_bitcast_fusion = f32[256,1280]{1,0:T(8,128)} fusion(bf16[2048,1280]{1,0:T(8,128)(2,1)} %all-gather.2.cloned.1.call-done, bf16[2048,256]{1,0:T(8,128)(2,1)S(1)} %bitcast.53), kind=kOutput, calls=%fused_computation.1 | convolution fusion | flops 1342177280 | bytes 7602176 | tf_op jit(solution)/shard_map/dot_general | solution.py:179
  140.0 4.8 %all-to-all-done.5.whole_ref = f32[32,8,128]{2,1,0:T(8,128)S(1)} async-done(((f32[32,8,128]{2,1,0:T(8,128)}), f32[32,8,128]{2,1,0:T(8,128)S(1)}, u32[]{:S(2)}, u32[]{:S(2)}) %all-to-all-start.5) | async-done | bytes 131104 | tf_op jit(solution)/shard_map/all_to_all | solution.py:117
  144.8 1.5 shard_map.78
  146.2 0.0 copy-start.2
  146.3 0.5 fusion.19
  146.8 0.0 collective-permute-done.3
  146.8 0.8 copy-done.2
  147.6 0.6 fusion.2
  148.2 1.1 maximum_bitcast_fusion
  (7 shorter events, 0.1 us)
Async XLA Ops:
  10.9 20.5 %copy-start.5 = (bf16[128,1280]{1,0:T(8,128)(2,1)S(1)}, bf16[128,1280]{1,0:T(8,128)(2,1)}, u32[]{:S(2)}) copy-start(bf16[128,1280]{1,0:T(8,128)(2,1)} %get-tuple-element.21) | copy-start | bytes 983044
  10.9 21.5 %all-to-all-start = ((f32[16,8,128]{2,1,0:T(8,128)}), f32[16,8,128]{2,1,0:T(8,128)S(1)}, u32[]{:S(2)}, u32[]{:S(2)}) async-start(f32[16,8,128]{2,1,0:T(8,128)} %get-tuple-element.20), calls=%async_computation | async-start | bytes 131072 | tf_op jit(solution)/shard_map/all_to_all | solution.py:117
  21.3 97.1 %all-gather.2.cloned.1.call-start = ((), (), s32[]{:S(2)}) async-start(), calls=%async_computation.6 | async-start | bytes 5898240 | tf_op jit(solution)/shard_map/all_gather | solution.py:148
  21.3 10.1 %collective-permute-start = (bf16[128,1280]{1,0:T(8,128)(2,1)}, bf16[128,1280]{1,0:T(8,128)(2,1)S(1)}, u32[]{:S(2)}, u32[]{:S(2)}) collective-permute-start(bf16[128,1280]{1,0:T(8,128)(2,1)} %get-tuple-element.22), channel_id=1, source_target_pairs={{0,384},{384,0},{1,385},{385,1},{2,386},{386,2},{3,387},{387,3},{4... | collective-permute-start | bytes 983048 | tf_op jit(solution)/shard_map/ppermute | solution.py:143
  31.5 1.5 copy-start.1
  40.9 28.7 %all-to-all-start.1 = ((f32[48,8,128]{2,1,0:T(8,128)}), f32[48,8,128]{2,1,0:T(8,128)}, u32[]{:S(2)}, u32[]{:S(2)}) async-start(f32[48,8,128]{2,1,0:T(8,128)} %broadcast_in_dim.12), calls=%async_computation.1 | async-start | bytes 393216 | tf_op jit(solution)/shard_map/all_to_all | solution.py:117
  56.5 24.9 %copy-start = (bf16[1,256,2560]{2,1,0:T(8,128)(2,1)S(1)}, bf16[1,256,2560]{2,1,0:T(8,128)(2,1)}, u32[]{:S(2)}) copy-start(bf16[1,256,2560]{2,1,0:T(8,128)(2,1)} %param.10) | copy-start | bytes 3932164
  57.6 60.7 %collective-permute-start.1 = (bf16[1024,256]{1,0:T(8,128)(2,1)}, bf16[1024,256]{1,0:T(8,128)(2,1)}, u32[]{:S(2)}, u32[]{:S(2)}) collective-permute-start(bf16[1024,256]{1,0:T(8,128)(2,1)} %get-tuple-element.40), channel_id=1, source_target_pairs={{0,384},{384,0},{1,385},{385,1},{2,386},{386,2},{3,387},{387,3},{4... | collective-permute-start | bytes 1572872 | tf_op jit(solution)/shard_map/ppermute | solution.py:153
  72.1 10.6 %copy-start.4 = (bf16[1024,256]{1,0:T(8,128)(2,1)S(1)}, bf16[1024,256]{1,0:T(8,128)(2,1)}, u32[]{:S(2)}) copy-start(bf16[1024,256]{1,0:T(8,128)(2,1)} %get-tuple-element.30) | copy-start | bytes 1572868
  72.1 19.2 %copy-start.3 = (bf16[128,2560]{1,0:T(8,128)(2,1)S(1)}, bf16[128,2560]{1,0:T(8,128)(2,1)}, u32[]{:S(2)}) copy-start(bf16[128,2560]{1,0:T(8,128)(2,1)} %get-tuple-element.27) | copy-start | bytes 1966084
  72.1 18.4 %all-to-all-start.2 = ((f32[16,8,128]{2,1,0:T(8,128)}), f32[16,8,128]{2,1,0:T(8,128)}, u32[]{:S(2)}, u32[]{:S(2)}) async-start(f32[16,8,128]{2,1,0:T(8,128)} %convolution_bitcast_fusion.1), calls=%async_computation.2 | async-start | bytes 131072 | tf_op jit(solution)/shard_map/all_to_all | solution.py:117
  82.7 35.6 %collective-permute-start.2 = (bf16[1024,256]{1,0:T(8,128)(2,1)S(1)}, bf16[1024,256]{1,0:T(8,128)(2,1)}, u32[]{:S(2)}, u32[]{:S(2)}) collective-permute-start(bf16[1024,256]{1,0:T(8,128)(2,1)S(1)} %copy-done.4), channel_id=1, source_target_pairs={{0,384},{384,0},{1,385},{385,1},{2,386},{386,2},{3,387},{387,3},{4... | collective-permute-start | bytes 1572872 | tf_op jit(solution)/shard_map/ppermute | solution.py:163
  111.0 18.4 %all-to-all-start.4 = ((f32[24,8,128]{2,1,0:T(8,128)}), f32[24,8,128]{2,1,0:T(8,128)}, u32[]{:S(2)}, u32[]{:S(2)}) async-start(f32[24,8,128]{2,1,0:T(8,128)} %broadcast_in_dim.30), calls=%async_computation.4 | async-start | bytes 196608 | tf_op jit(solution)/shard_map/all_to_all | solution.py:117
  123.6 23.2 %collective-permute-start.3 = (bf16[256,1280]{1,0:T(8,128)(2,1)}, bf16[256,1280]{1,0:T(8,128)(2,1)S(1)}, u32[]{:S(2)}, u32[]{:S(2)}) collective-permute-start(bf16[256,1280]{1,0:T(8,128)(2,1)} %convolution_convert_fusion), channel_id=1, source_target_pairs={{0,384},{384,0},{1,385},{385,1},{2,386},{386,2},{3,387},{387,3},{4... | collective-permute-start | bytes 1966088 | tf_op jit(solution)/shard_map/ppermute | solution.py:176
  131.0 13.8 %all-to-all-start.5 = ((f32[32,8,128]{2,1,0:T(8,128)}), f32[32,8,128]{2,1,0:T(8,128)S(1)}, u32[]{:S(2)}, u32[]{:S(2)}) async-start(f32[32,8,128]{2,1,0:T(8,128)} %broadcast_in_dim.31), calls=%async_computation.5 | async-start | bytes 262144 | tf_op jit(solution)/shard_map/all_to_all | solution.py:117
  146.2 1.3 copy-start.2
Sparse Core Ops, SparseCore 0:
  32.6 83.2 all-gather.1
